TPU v7x, 512 devices: a whole 4x4x16 slice. The times are simulated.
512 devices in a mesh: ctx: 64 (over x_lo, z, core), dp: 8 (over y, x_hi).
Axes of the slice: x: 4 (x_hi: 2, x_lo: 2; x = x_hi * 2 + x_lo), y: 4, z: 16, core: 2. Of those that a mesh axis runs over, the one named last changes fastest.
Arguments:
- query_states: bfloat16 [8, 8192, 2048], P('dp', 'ctx'), may hold values from -6 to 6
- key_activations: bfloat16 [8, 8192, 512], P('dp', 'ctx'), may hold values from -6 to 6
- value_activations: bfloat16 [8, 8192, 512], P('dp', 'ctx'), may hold values from -6 to 6
- out_grad: bfloat16 [8, 8192, 2048], P('dp', 'ctx'), may hold values from -6 to 6
- logsumexp: bfloat16 [8, 16, 8192], P('dp', None, 'ctx'), may hold values from 4 to 5
- row_delta: bfloat16 [8, 16, 8192], P('dp', None, 'ctx'), may hold values from -1 to 1
- layer_input: bfloat16 [8, 8192, 2048], P('dp', 'ctx'), may hold values from -16 to 16
- chosen: int32 [8, 128, 4, 3], P('dp', 'ctx'), may hold values from -1 to 125, as said below
Outputs:
- query_grad: bfloat16 [8, 8192, 2048], P('dp', 'ctx')
- key_gradient: bfloat16 [8, 8192, 512], P('dp', 'ctx')
- value_gradient: bfloat16 [8, 8192, 512], P('dp', 'ctx')
- key_weight_grad: float32 [2048, 512], P(('ctx', 'dp'))
Inputs may be any that keep to these rules, and one draw needn't show every extreme that they name: `chosen`: -1 marks an unused choice. Every other entry names a block of an earlier shard of 128 positions of the same sequence; the 3 used entries of one query block and key-value head differ. The used entries of the query blocks of one shard name blocks of one other shard at most 2 times, and exactly 2 times for some pair of shards.
All inputs are finite; a program needn't handle non-finite values.
Results may differ from a plain program's by a relative error of at most 0.0052.
Values may be sent and summed in bfloat16 or wider, within the bound.
A program may use at most 192 MiB of HBM per device.

v0:
```python
import math

import jax
import jax.numpy as jnp
from jax import lax
from jax.sharding import PartitionSpec as P

HEAD_WIDTH = 128
BLOCK_LENGTH = 64
CHOSEN_BLOCKS = 3
CAP = 2


def assign_slots(choices_flat, shards, per_shard, slot_count, kv_heads):
    request_number = choices_flat.shape[0]
    active = choices_flat >= 0
    owners = jnp.where(active, choices_flat // per_shard, -1)
    positions = jnp.arange(request_number, dtype=jnp.int32)
    earlier = positions[None, :] < positions[:, None]
    same_owner = (owners[:, None] == owners[None, :]) & active[None, :] & earlier
    ranking = jnp.sum(same_owner.astype(jnp.int32), axis=1)
    slot_index = jnp.where(active, owners * slot_count + ranking, -1)
    head_index = positions // CHOSEN_BLOCKS % kv_heads
    unit_index = jnp.where(active, choices_flat % per_shard * kv_heads + head_index, -1)
    matches = (
        slot_index[:, None] == jnp.arange(shards * slot_count, dtype=jnp.int32)[None, :]
    ).astype(jnp.int32)
    filled = jnp.sum(matches, axis=0) > 0
    slot_request = jnp.where(filled, jnp.sum(matches * positions[:, None], axis=0), -1)
    slot_unit = jnp.where(filled, jnp.sum(matches * unit_index[:, None], axis=0), -1)
    return (slot_index, active, slot_request, slot_unit)


def block_grads(
    keys_blk, values_blk, rows_blk, grads_blk, lse_blk, delta_blk, valid_mask, score_scale
):
    scores = (
        jnp.einsum("...kd,...rd->...kr", keys_blk, rows_blk, preferred_element_type=jnp.float32)
        * score_scale
    )
    prob_vals = jnp.where(valid_mask, jnp.exp(scores - lse_blk[..., None, :]), 0.0)
    dprob_vals = jnp.einsum(
        "...kd,...rd->...kr", values_blk, grads_blk, preferred_element_type=jnp.float32
    )
    dscore_low = (prob_vals * (dprob_vals - delta_blk[..., None, :])).astype(jnp.bfloat16)
    prob_low = prob_vals.astype(jnp.bfloat16)
    row_grad = (
        jnp.einsum("...kr,...kd->...rd", dscore_low, keys_blk, preferred_element_type=jnp.float32)
        * score_scale
    )
    key_part = (
        jnp.einsum("...kr,...rd->...kd", dscore_low, rows_blk, preferred_element_type=jnp.float32)
        * score_scale
    )
    value_part = jnp.einsum(
        "...kr,...rd->...kd", prob_low, grads_blk, preferred_element_type=jnp.float32
    )
    return (row_grad, key_part, value_part)


def body(
    query_states,
    key_activations,
    value_activations,
    out_grad,
    logsumexp,
    row_delta,
    layer_input,
    chosen,
):
    shards = lax.axis_size("ctx")
    replicas = lax.axis_size("dp")
    tokens = query_states.shape[1]
    kv_heads = key_activations.shape[2] // HEAD_WIDTH
    head_group_width = query_states.shape[2] // key_activations.shape[2]
    per_shard = tokens // BLOCK_LENGTH
    row_number = head_group_width * BLOCK_LENGTH
    score_scale = HEAD_WIDTH ** (-0.5)
    slot_total = shards * CAP
    unit_total = per_shard * kv_heads
    query_rows = (
        query_states[0]
        .reshape(tokens, kv_heads, head_group_width, HEAD_WIDTH)
        .transpose(1, 2, 0, 3)
    )
    rowwise_gradient = (
        out_grad[0].reshape(tokens, kv_heads, head_group_width, HEAD_WIDTH).transpose(1, 2, 0, 3)
    )
    shard_key_rows = key_activations[0].reshape(tokens, kv_heads, HEAD_WIDTH).transpose(1, 0, 2)
    shard_value_rows = value_activations[0].reshape(tokens, kv_heads, HEAD_WIDTH).transpose(1, 0, 2)
    lse_low = logsumexp[0].reshape(kv_heads, head_group_width, tokens)
    delta_low = row_delta[0].reshape(kv_heads, head_group_width, tokens)
    rowwise_logsum = lse_low.astype(jnp.float32)
    rowwise_delta = delta_low.astype(jnp.float32)
    key_pos = jnp.arange(tokens, dtype=jnp.int32)
    causal = key_pos[:, None] <= jnp.tile(key_pos, head_group_width)[None, :]
    nearby_rows, nearby_keys, nearby_values = block_grads(
        shard_key_rows,
        shard_value_rows,
        query_rows.reshape(kv_heads, head_group_width * tokens, HEAD_WIDTH),
        rowwise_gradient.reshape(kv_heads, head_group_width * tokens, HEAD_WIDTH),
        rowwise_logsum.reshape(kv_heads, head_group_width * tokens),
        rowwise_delta.reshape(kv_heads, head_group_width * tokens),
        causal[None],
        score_scale,
    )
    blockwise_queries = (
        query_rows.reshape(kv_heads, head_group_width, per_shard, BLOCK_LENGTH, HEAD_WIDTH)
        .transpose(2, 0, 1, 3, 4)
        .reshape(per_shard, kv_heads, row_number, HEAD_WIDTH)
    )
    blockwise_gradient = (
        rowwise_gradient.reshape(kv_heads, head_group_width, per_shard, BLOCK_LENGTH, HEAD_WIDTH)
        .transpose(2, 0, 1, 3, 4)
        .reshape(per_shard, kv_heads, row_number, HEAD_WIDTH)
    )
    lse_low_blocks = (
        lse_low.reshape(kv_heads, head_group_width, per_shard, BLOCK_LENGTH)
        .transpose(2, 0, 1, 3)
        .reshape(per_shard, kv_heads, row_number)
    )
    delta_low_blocks = (
        delta_low.reshape(kv_heads, head_group_width, per_shard, BLOCK_LENGTH)
        .transpose(2, 0, 1, 3)
        .reshape(per_shard, kv_heads, row_number)
    )
    choices_flat = chosen[0].reshape(-1)
    slot_index, active, slot_request, slot_unit = assign_slots(
        choices_flat, shards, per_shard, CAP, kv_heads
    )
    served = lax.all_to_all(
        slot_unit.reshape(shards, CAP), "ctx", split_axis=0, concat_axis=0, tiled=True
    )
    served = served.reshape(slot_total)
    served_ok = served >= 0
    served_safe = jnp.maximum(served, 0)
    onehot = (served[None, :] == jnp.arange(unit_total, dtype=jnp.int32)[:, None]).astype(
        jnp.float32
    )
    block_units = (
        jnp.stack(
            [
                key_activations[0].reshape(per_shard, BLOCK_LENGTH, kv_heads, HEAD_WIDTH),
                value_activations[0].reshape(per_shard, BLOCK_LENGTH, kv_heads, HEAD_WIDTH),
            ],
            axis=3,
        )
        .transpose(0, 2, 1, 3, 4)
        .reshape(unit_total, BLOCK_LENGTH, 2, HEAD_WIDTH)
    )
    filled = slot_request >= 0
    outgoing = jnp.where(
        served_ok[:, None, None, None], jnp.take(block_units, served_safe, axis=0), 0.0
    )
    arrived = lax.all_to_all(
        outgoing.reshape(shards, CAP, BLOCK_LENGTH, 2, HEAD_WIDTH),
        "ctx",
        split_axis=0,
        concat_axis=0,
        tiled=True,
    )
    arrived = arrived.reshape(slot_total, BLOCK_LENGTH, 2, HEAD_WIDTH)
    fetched = jnp.take(arrived, jnp.maximum(slot_index, 0), axis=0).reshape(
        per_shard, kv_heads, CHOSEN_BLOCKS * BLOCK_LENGTH, 2, HEAD_WIDTH
    )
    valid_mask = jnp.repeat(
        active.reshape(per_shard, kv_heads, CHOSEN_BLOCKS), BLOCK_LENGTH, axis=2
    )[..., None]
    remote_row_list, remote_key_rows, remote_value_rows = block_grads(
        fetched[..., 0, :],
        fetched[..., 1, :],
        blockwise_queries,
        blockwise_gradient,
        lse_low_blocks.astype(jnp.float32),
        delta_low_blocks.astype(jnp.float32),
        valid_mask,
        score_scale,
    )
    partials = jnp.stack([remote_key_rows, remote_value_rows], axis=3).reshape(
        unit_total * CHOSEN_BLOCKS, BLOCK_LENGTH, 2, HEAD_WIDTH
    )
    outgoing_back = jnp.where(
        filled[:, None, None, None], jnp.take(partials, jnp.maximum(slot_request, 0), axis=0), 0.0
    )
    returned = lax.all_to_all(
        outgoing_back.reshape(shards, CAP, BLOCK_LENGTH, 2, HEAD_WIDTH),
        "ctx",
        split_axis=0,
        concat_axis=0,
        tiled=True,
    )
    unit_sums = jnp.dot(
        onehot,
        returned.reshape(slot_total, BLOCK_LENGTH * 2 * HEAD_WIDTH),
        precision=lax.Precision.HIGHEST,
    )
    remote_row_list = remote_row_list.reshape(
        per_shard, kv_heads, head_group_width, BLOCK_LENGTH, HEAD_WIDTH
    ).transpose(1, 2, 0, 3, 4)
    overall_rows = nearby_rows + remote_row_list.reshape(
        kv_heads, head_group_width * tokens, HEAD_WIDTH
    )
    query_grad = overall_rows.reshape(kv_heads, head_group_width, tokens, HEAD_WIDTH).transpose(
        2, 0, 1, 3
    )
    query_grad = query_grad.reshape(1, tokens, kv_heads * head_group_width * HEAD_WIDTH).astype(
        jnp.bfloat16
    )
    far_units = (
        unit_sums.reshape(per_shard, kv_heads, BLOCK_LENGTH, 2, HEAD_WIDTH)
        .transpose(1, 0, 2, 3, 4)
        .reshape(kv_heads, tokens, 2, HEAD_WIDTH)
    )
    key_total = nearby_keys + far_units[:, :, 0]
    value_total = nearby_values + far_units[:, :, 1]
    key_gradient = (
        key_total.transpose(1, 0, 2).reshape(1, tokens, kv_heads * HEAD_WIDTH).astype(jnp.bfloat16)
    )
    value_gradient = (
        value_total.transpose(1, 0, 2)
        .reshape(1, tokens, kv_heads * HEAD_WIDTH)
        .astype(jnp.bfloat16)
    )
    inputs_flat = layer_input[0]
    key_flat = key_gradient[0]
    weight_scale = 1.0 / math.sqrt(tokens * shards * replicas)
    key_weight_grad = lax.psum_scatter(
        jnp.einsum("td,tk->dk", inputs_flat, key_flat, preferred_element_type=jnp.float32)
        * weight_scale,
        ("ctx", "dp"),
        scatter_dimension=0,
        tiled=True,
    )
    return (query_grad, key_gradient, value_gradient, key_weight_grad)


def solution(mesh):
    in_specs = (
        P("dp", "ctx", None),
        P("dp", "ctx", None),
        P("dp", "ctx", None),
        P("dp", "ctx", None),
        P("dp", None, "ctx"),
        P("dp", None, "ctx"),
        P("dp", "ctx", None),
        P("dp", "ctx", None, None),
    )
    out_specs = (
        P("dp", "ctx", None),
        P("dp", "ctx", None),
        P("dp", "ctx", None),
        P(("ctx", "dp"), None),
    )
    return jax.shard_map(body, mesh=mesh, in_specs=in_specs, out_specs=out_specs, check_vma=False)
```

profile of v0, /device:TPU:24, one launch (start us, length us, event | category | flops | bytes accessed | tf_op | source)
XLA Modules:
  0.0 1171.4 jit_solution(16199561269067164148)
XLA Ops:
  7.2 0.8 copy.176
  8.4 0.8 select_n.196
  9.2 17.0 %all-to-all-start = ((s32[64,1,2]{2,1,0:T(1,128)}), s32[64,1,2]{2,1,0:T(1,128)S(1)}, u32[]{:S(2)}, u32[]{:S(2)}) async-start(s32[64,1,2]{2,1,0:T(1,128)} %bitcast.6), calls=%async_computation | async-start | bytes 65536 | tf_op jit(solution)/shard_map/all_to_all | solution.py:131
  26.2 0.9 stack_reshape_squeeze.6
  27.2 0.9 stack_reshape_squeeze.7
  28.4 11.2 all-to-all-done
  40.1 3.1 gather_fusion
  43.2 3.9 select_select_fusion.1
  47.1 5.8 all-to-all-start.1
  55.6 186.0 %all-to-all-done.1 = bf16[64,2,64,2,128]{4,2,3,1,0:T(8,128)(2,1)} async-done(((bf16[64,2,64,2,128]{4,2,3,1,0:T(8,128)(2,1)}), bf16[64,2,64,2,128]{4,2,3,1,0:T(8,128)(2,1)}, u32[]{:S(2)}, u32[]{:S(2)}) %all-to-all-start.1) | async-done | bytes 4194336 | tf_op jit(solution)/shard_map/all_to_all | solution.py:155
  241.6 2.9 gather_fusion.1
  247.1 4.3 gather_fusion.2
  251.5 14.3 %copy.194 = f32[128,64,2,128]{3,2,1,0:T(2,128)S(1)} copy(f32[128,64,2,128]{3,1,2,0:T(8,128)} %gather_fusion.2) | data formatting | bytes 16777216 | tf_op jit(solution)/shard_map/jit(_take)/gather | solution.py:183
  265.8 6.8 select_select_fusion
  272.6 6.3 all-to-all-start.2
  279.9 0.7 reshape_squeeze.23
  283.2 1.0 copy-done.3
  284.2 1.2 fusion.5
  285.9 1.5 reduce.3
  287.5 357.2 %all-to-all-done.2 = f32[64,2,64,2,128]{4,3,2,1,0:T(2,128)} async-done(((f32[64,2,64,2,128]{4,3,2,1,0:T(2,128)}), f32[64,2,64,2,128]{4,3,2,1,0:T(2,128)}, u32[]{:S(2)}, u32[]{:S(2)}) %all-to-all-start.2) | async-done | bytes 8388640 | tf_op jit(solution)/shard_map/all_to_all | solution.py:185
  644.7 11.5 reshape.536
  656.2 9.0 copy.195
  665.3 7.2 convolution_bitcast_fusion
  672.6 0.8 fusion.32
  673.8 2.7 multiply_bitcast_fusion
  676.5 1.5 convolution_multiply_fusion
  678.9 1.2 convert_element_type.151
  680.6 0.8 copy.200
  681.4 0.8 copy.199
  682.1 480.6 %all-reduce.3.cloned.1.call-done = f32[2048,512]{0,1:T(8,128)} async-done(((f32[2048,512]{0,1:T(8,128)}), f32[2048,512]{0,1:T(8,128)}) %all-reduce.3.cloned.1.call-update) | async-done | bytes 4194320
  1162.7 1.1 constant_dynamic-slice_fusion
  1163.8 0.7 copy.201
  (114 shorter events, 12.3 us)
Async XLA Ops:
  7.2 666.6 %copy-start = (bf16[1,128,2048]{2,1,0:T(8,128)(2,1)S(1)}, bf16[1,128,2048]{2,1,0:T(8,128)(2,1)}, u32[]{:S(2)}) copy-start(bf16[1,128,2048]{2,1,0:T(8,128)(2,1)} %param.14) | copy-start | bytes 1572868
  9.2 30.4 %all-to-all-start = ((s32[64,1,2]{2,1,0:T(1,128)}), s32[64,1,2]{2,1,0:T(1,128)S(1)}, u32[]{:S(2)}, u32[]{:S(2)}) async-start(s32[64,1,2]{2,1,0:T(1,128)} %bitcast.6), calls=%async_computation | async-start | bytes 65536 | tf_op jit(solution)/shard_map/all_to_all | solution.py:131
  39.5 3.7 copy-start.15
  47.1 6.1 copy-start.18
  47.1 6.7 copy-start.11
  47.1 7.2 copy-start.16
  47.1 7.4 copy-start.12
  47.1 194.6 %all-to-all-start.1 = ((bf16[64,2,64,2,128]{4,2,3,1,0:T(8,128)(2,1)}), bf16[64,2,64,2,128]{4,2,3,1,0:T(8,128)(2,1)}, u32[]{:S(2)}, u32[]{:S(2)}) async-start(bf16[64,2,64,2,128]{4,2,3,1,0:T(8,128)(2,1)} %select_select_fusion.1), calls=%async_computation.1 | async-start | bytes 8388608 | tf_op jit(solution)/shard_map/all_to_all | solution.py:155
  52.9 2.1 copy-start.17
  54.3 191.2 %copy-start.6 = (bf16[4,4,2,64,128]{4,3,1,0,2:T(8,128)(2,1)}, bf16[4,4,2,64,128]{4,3,1,0,2:T(8,128)(2,1)S(1)}, u32[]{:S(2)}) copy-start(bf16[4,4,2,64,128]{4,3,1,0,2:T(8,128)(2,1)S(1)} %copy.188) | copy-start | bytes 1572868
  54.9 190.7 %copy-start.1 = (bf16[128,4,4,128]{3,2,1,0:T(4,128)(2,1)}, bf16[128,4,4,128]{3,2,1,0:T(4,128)(2,1)S(1)}, u32[]{:S(2)}) copy-start(bf16[128,4,4,128]{3,2,1,0:T(4,128)(2,1)S(1)} %reshape_squeeze.24) | copy-start | bytes 1572868
  244.9 1.5 copy-start.5
  245.6 1.0 copy-start.7
  272.6 6.6 copy-start.13
  272.6 7.3 copy-start.14
  272.6 8.8 copy-start.2
  272.6 372.1 %all-to-all-start.2 = ((f32[64,2,64,2,128]{4,3,2,1,0:T(2,128)}), f32[64,2,64,2,128]{4,3,2,1,0:T(2,128)}, u32[]{:S(2)}, u32[]{:S(2)}) async-start(f32[64,2,64,2,128]{4,3,2,1,0:T(2,128)} %select_select_fusion), calls=%async_computation.2 | async-start | bytes 16777216 | tf_op jit(solution)/shard_map/all_to_all | solution.py:185
  278.9 883.8 %all-reduce.3.cloned.1.call-start = ((), (), s32[]{:S(2)}) async-start(), calls=%async_computation.3 | async-start | bytes 8388608
  279.2 6.1 copy-start.9
  280.6 2.2 copy-start.19
  283.2 1.0 copy-start.3
  656.2 9.0 copy-start.20
  676.4 1.7 copy-start.10
  676.5 3.6 copy-start.8
  678.0 2.2 copy-start.4
Sparse Core Ops, SparseCore 0:
  676.6 486.0 all-reduce.2
where the time goes:
time: 1170 us
  waiting for transfers between devices  1040 us (89%)
  local copies, waits for them, and re-layouts  62.8 us (5%)
  starting transfers between devices  29.4 us (3%)
  matrix products  15.7 us (1%)
  between operations  14.6 us (1%)
  other arithmetic  13.8 us (1%)
    unnamed x2, waiting for transfers between devices  481 us
    all_to_all x1, waiting for transfers between devices, body(): lax.all_to_all(outgoing_back.reshape(shards, CAP, BLOCK_LENGTH, 2, HEAD_W...  357 us
    all_to_all x1, waiting for transfers between devices, body(): lax.all_to_all(outgoing.reshape(shards, CAP, BLOCK_LENGTH, 2, HEAD_WIDTH)...  186 us
  transfers between devices with their start and end apart: 4, of which 4 were waited for; matrix products, arithmetic and copies ran while one was open for 1% of the time, Pallas kernels for 0%

commit v1 on v0

v1 whole, which is shorter than its diff:
```python
import functools
import math

import jax
import jax.numpy as jnp
from jax import lax
from jax.experimental import pallas as pl
from jax.experimental.pallas import tpu as pltpu
from jax.sharding import PartitionSpec as P

HEAD_WIDTH = 128
BLOCK_LENGTH = 64
CHOSEN_BLOCKS = 3
CAP = 2
KV_HEADS = 4
GROUP = 4
TOKENS = 128
UNITS = TOKENS // BLOCK_LENGTH * KV_HEADS
PAIR = 2 * HEAD_WIDTH
MESH = pl.DeviceIdType.MESH


def place(ring):
    i = lax.axis_index("ctx")
    return i // (2 * ring), lax.rem(i // 2, ring), lax.rem(i, 2)


def member(ring, j):
    x, z, c = place(ring)
    mx = lax.rem(x + j // 2, 2)
    mc = lax.rem(c + j % 2, 2)
    return mx * (2 * ring) + z * 2 + mc, mx * 2 + mc


def along(ring, step):
    x, z, c = place(ring)
    return x * (2 * ring) + lax.rem(z + step + ring, ring) * 2 + c


def greet(ring):
    barrier = pltpu.get_barrier_semaphore()
    for other in (along(ring, 1), along(ring, -1)) + tuple(member(ring, j)[0] for j in (1, 2, 3)):
        pl.semaphore_signal(barrier, inc=1, device_id={"ctx": other}, device_id_type=MESH)
    pl.semaphore_wait(barrier, 5)


def push(src, dst, send, recv, other):
    return pltpu.make_async_remote_copy(
        src_ref=src, dst_ref=dst, send_sem=send, recv_sem=recv,
        device_id={"ctx": other}, device_id_type=MESH,
    )


def gather_kernel(
    ring, k_ref, v_ref, want_ref, slots_ref, wants_ref,
    up, down, stage, work, want_smem,
    up_send, up_recv, down_send, down_recv, w_send, w_recv, s_send, s_recv, local_sem, smem_sem,
):
    half = ring // 2
    x, z, c = place(ring)
    cls = x * 2 + c
    above, below = along(ring, 1), along(ring, -1)
    greet(ring)

    def up_copy(s, part, src=None):
        src = up.at[s - 1, part] if src is None else src
        return push(src, up.at[s, part], up_send.at[s, part], up_recv.at[s, part], above)

    def down_copy(s, part, src=None):
        src = down.at[s - 1, part] if src is None else src
        return push(src, down.at[s, part], down_send.at[s, part], down_recv.at[s, part], below)

    def want_copy(j):
        other, other_cls = member(ring, j)
        return push(want_ref.at[other_cls], wants_ref.at[j], w_send.at[j - 1], w_recv.at[j - 1], other)

    for j in (1, 2, 3):
        want_copy(j).start()
    for part, ref in ((0, k_ref), (1, v_ref)):
        up_copy(0, part, ref).start()
        down_copy(0, part, ref).start()

    own = pltpu.make_async_copy(want_ref.at[cls], wants_ref.at[0], smem_sem)
    own.start()
    own.wait()
    for j in (1, 2, 3):
        want_copy(j).wait()
    table = pltpu.make_async_copy(wants_ref, want_smem, smem_sem)
    table.start()
    table.wait()

    def slot_copy(j, r):
        owner = lax.rem(z + r, ring)
        return push(
            stage.at[r, j], slots_ref.at[cls, owner], s_send.at[j - 1, r], s_recv.at[j - 1, r],
            member(ring, j)[0],
        )

    def own_copy(r):
        return pltpu.make_async_copy(
            stage.at[r, 0], slots_ref.at[cls, lax.rem(z + r, ring)], local_sem.at[r]
        )

    def extract(r, keys, values):
        owner = lax.rem(z + r, ring)
        for b in range(2):
            for h in range(KV_HEADS):
                rows, lanes = pl.ds(b * BLOCK_LENGTH, BLOCK_LENGTH), pl.ds(h * HEAD_WIDTH, HEAD_WIDTH)
                work[b * KV_HEADS + h, :, :HEAD_WIDTH] = keys[rows, lanes]
                work[b * KV_HEADS + h, :, HEAD_WIDTH:] = values[rows, lanes]
        for j in range(4):
            for rank in range(CAP):
                unit = jnp.maximum(want_smem[j, 0, owner * CAP + rank], 0)
                stage[r, j, rank] = work[unit]
        for j in (1, 2, 3):
            slot_copy(j, r).start()
        own_copy(r).start()

    extract(0, k_ref, v_ref)

    def step(s, _):
        for part in range(2):
            up_copy(s, part, k_ref).wait_recv()
            up_copy(s + 1, part).start()
            down_copy(s, part, k_ref).wait_recv()
            down_copy(s + 1, part).start()
        extract(ring - 1 - s, up.at[s, 0], up.at[s, 1])
        extract(1 + s, down.at[s, 0], down.at[s, 1])
        return 0

    lax.fori_loop(0, half - 2, step, 0)
    s = half - 2
    for part in range(2):
        up_copy(s, part, k_ref).wait_recv()
        if part == 0:
            up_copy(s + 1, part).start()
        down_copy(s, part, k_ref).wait_recv()
        if part == 1:
            down_copy(s + 1, part).start()
    extract(ring - 1 - s, up.at[s, 0], up.at[s, 1])
    extract(1 + s, down.at[s, 0], down.at[s, 1])
    up_copy(half - 1, 0, k_ref).wait_recv()
    down_copy(half - 1, 1, k_ref).wait_recv()
    extract(half, up.at[half - 1, 0], down.at[half - 1, 1])

    def drain(s, _):
        for part in range(2):
            up_copy(s, part, k_ref).wait_send()
            down_copy(s, part, k_ref).wait_send()
        return 0

    lax.fori_loop(0, half - 1, drain, 0)
    up_copy(half - 1, 0, k_ref).wait_send()
    down_copy(half - 1, 1, k_ref).wait_send()

    def drain_slots(r, _):
        for j in (1, 2, 3):
            slot_copy(j, r).wait()
        own_copy(r).wait()
        return 0

    lax.fori_loop(0, ring, drain_slots, 0)


def gather_call(ring, keys, values, want):
    half = ring // 2
    ring_buffer = pltpu.VMEM((half, 2, TOKENS, KV_HEADS * HEAD_WIDTH), jnp.bfloat16)
    ring_sem = pltpu.SemaphoreType.DMA((half, 2))
    return pl.pallas_call(
        functools.partial(gather_kernel, ring),
        out_shape=(
            jax.ShapeDtypeStruct((4, ring, CAP, BLOCK_LENGTH, PAIR), jnp.bfloat16),
            jax.ShapeDtypeStruct((4, 8, 128), jnp.int32),
        ),
        in_specs=[pl.BlockSpec(memory_space=pltpu.VMEM)] * 3,
        out_specs=(pl.BlockSpec(memory_space=pl.ANY), pl.BlockSpec(memory_space=pltpu.VMEM)),
        scratch_shapes=[
            ring_buffer,
            ring_buffer,
            pltpu.VMEM((ring, 4, CAP, BLOCK_LENGTH, PAIR), jnp.bfloat16),
            pltpu.VMEM((UNITS, BLOCK_LENGTH, PAIR), jnp.bfloat16),
            pltpu.SMEM((4, 8, 128), jnp.int32),
            ring_sem, ring_sem, ring_sem, ring_sem,
            pltpu.SemaphoreType.DMA((3,)),
            pltpu.SemaphoreType.DMA((3,)),
            pltpu.SemaphoreType.DMA((3, ring)),
            pltpu.SemaphoreType.DMA((3, ring)),
            pltpu.SemaphoreType.DMA((ring,)),
            pltpu.SemaphoreType.DMA,
        ],
        compiler_params=pltpu.CompilerParams(
            collective_id=0, has_side_effects=True, vmem_limit_bytes=40 * 1024 * 1024
        ),
        name="gather_blocks",
    )(keys, values, want)


def reduce_kernel(
    ring, part_ref, wants_ref, dk_ref, dv_ref, kg_ref, vg_ref,
    up, down, ups, downs, arrived, want_smem,
    up_send, up_recv, down_send, down_recv, s_send, s_recv, smem_sem,
):
    half = ring // 2
    x, z, c = place(ring)
    cls = x * 2 + c
    above, below = along(ring, 1), along(ring, -1)
    greet(ring)

    def slot_copy(j, r):
        other, other_cls = member(ring, j)
        owner = lax.rem(z + r, ring)
        return push(
            part_ref.at[other_cls, owner], arrived.at[j - 1, r],
            s_send.at[j - 1, r], s_recv.at[j - 1, r], other,
        )

    for j in (1, 2, 3):
        slot_copy(j, half).start()

    def send_slots(s, _):
        for j in (1, 2, 3):
            slot_copy(j, half - s).start()
            slot_copy(j, half + s).start()
        return 0

    lax.fori_loop(1, half, send_slots, 0)
    for j in (1, 2, 3):
        slot_copy(j, 0).start()
    table = pltpu.make_async_copy(wants_ref, want_smem, smem_sem)
    table.start()
    blank = jnp.zeros((TOKENS, KV_HEADS * HEAD_WIDTH), jnp.bfloat16)
    up[0, 1] = blank
    down[0, 0] = blank
    table.wait()

    def up_copy(s, part):
        return push(ups.at[s, part], up.at[s, part], up_send.at[s, part], up_recv.at[s, part], above)

    def down_copy(s, part):
        return push(
            downs.at[s, part], down.at[s, part], down_send.at[s, part], down_recv.at[s, part], below
        )

    def total(r, part, incoming, target):
        owner = lax.rem(z + r, ring)
        lanes = pl.ds(part * HEAD_WIDTH, HEAD_WIDTH)
        units = [[want_smem[j, 0, owner * CAP + rank] for rank in range(CAP)] for j in range(4)]
        for b in range(2):
            for h in range(KV_HEADS):
                at = (pl.ds(b * BLOCK_LENGTH, BLOCK_LENGTH), pl.ds(h * HEAD_WIDTH, HEAD_WIDTH))
                acc = jnp.zeros((BLOCK_LENGTH, HEAD_WIDTH), jnp.float32)
                for ref in incoming:
                    acc = acc + ref[at].astype(jnp.float32)
                for j in range(4):
                    for rank in range(CAP):
                        if j == 0:
                            term = part_ref[cls, owner, rank, :, lanes]
                        else:
                            term = arrived[j - 1, r, rank, :, lanes]
                        hit = units[j][rank] == b * KV_HEADS + h
                        acc = acc + jnp.where(hit, term.astype(jnp.float32), 0.0)
                target[at] = acc.astype(jnp.bfloat16)

    for j in (1, 2, 3):
        slot_copy(j, half).wait_recv()
    total(half, 0, [], ups.at[0, 0])
    up_copy(0, 0).start()
    total(half, 1, [], downs.at[0, 1])
    down_copy(0, 1).start()

    def step(s, _):
        for j in (1, 2, 3):
            slot_copy(j, half - s).wait_recv()
            slot_copy(j, half + s).wait_recv()

        up_copy(s - 1, 0).wait_recv()
        total(half - s, 0, [up.at[s - 1, 0]], ups.at[s, 0])
        up_copy(s, 0).start()
        down_copy(s - 1, 1).wait_recv()
        total(half + s, 1, [down.at[s - 1, 1]], downs.at[s, 1])
        down_copy(s, 1).start()

        @pl.when(s > 1)
        def _():
            up_copy(s - 1, 1).wait_recv()
            down_copy(s - 1, 0).wait_recv()

        total(half - s, 1, [up.at[s - 1, 1]], ups.at[s, 1])
        up_copy(s, 1).start()
        total(half + s, 0, [down.at[s - 1, 0]], downs.at[s, 0])
        down_copy(s, 0).start()
        return 0

    lax.fori_loop(1, half, step, 0)
    for j in (1, 2, 3):
        slot_copy(j, 0).wait_recv()
    for part, near, out in ((0, dk_ref, kg_ref), (1, dv_ref, vg_ref)):
        up_copy(half - 1, part).wait_recv()
        down_copy(half - 1, part).wait_recv()
        total(0, part, [near, up.at[half - 1, part], down.at[half - 1, part]], out)

    up_copy(0, 0).wait_send()
    down_copy(0, 1).wait_send()

    def drain(s, _):
        for part in range(2):
            up_copy(s, part).wait_send()
            down_copy(s, part).wait_send()
        return 0

    lax.fori_loop(1, half, drain, 0)

    def drain_slots(r, _):
        for j in (1, 2, 3):
            slot_copy(j, r).wait_send()
        return 0

    lax.fori_loop(0, ring, drain_slots, 0)


def reduce_call(ring, parts, wants, dk, dv):
    half = ring // 2
    width = KV_HEADS * HEAD_WIDTH
    ring_buffer = pltpu.VMEM((half, 2, TOKENS, width), jnp.bfloat16)
    ring_sem = pltpu.SemaphoreType.DMA((half, 2))
    return pl.pallas_call(
        functools.partial(reduce_kernel, ring),
        out_shape=(jax.ShapeDtypeStruct((TOKENS, width), jnp.bfloat16),) * 2,
        in_specs=[pl.BlockSpec(memory_space=pltpu.VMEM)] * 4,
        out_specs=(pl.BlockSpec(memory_space=pltpu.VMEM),) * 2,
        scratch_shapes=[
            ring_buffer, ring_buffer, ring_buffer, ring_buffer,
            pltpu.VMEM((3, ring, CAP, BLOCK_LENGTH, PAIR), jnp.bfloat16),
            pltpu.SMEM((4, 8, 128), jnp.int32),
            ring_sem, ring_sem, ring_sem, ring_sem,
            pltpu.SemaphoreType.DMA((3, ring)),
            pltpu.SemaphoreType.DMA((3, ring)),
            pltpu.SemaphoreType.DMA,
        ],
        compiler_params=pltpu.CompilerParams(
            collective_id=1, has_side_effects=True, vmem_limit_bytes=40 * 1024 * 1024
        ),
        name="reduce_blocks",
    )(parts, wants, dk, dv)


def attend_kernel(
    place_ref, valid_ref, q_ref, g_ref, k_ref, v_ref, lse_ref, delta_ref, f0, f1, f2,
    dq_ref, dk_ref, dv_ref, part_ref,
):
    h, b = pl.program_id(0), pl.program_id(1)
    scale = HEAD_WIDTH ** (-0.5)
    first = (b * KV_HEADS + h) * CHOSEN_BLOCKS
    fetched = (f0, f1, f2)
    local = TOKENS
    keys_n = local + CHOSEN_BLOCKS * BLOCK_LENGTH
    rows_n = GROUP * BLOCK_LENGTH

    @pl.when((h == 0) & (b == 0))
    def _():
        part_ref[...] = jnp.zeros_like(part_ref)

    def stack(ref):
        return jnp.concatenate(
            [ref[:, i * HEAD_WIDTH : (i + 1) * HEAD_WIDTH] for i in range(GROUP)], axis=0
        )

    queries, grads = stack(q_ref), stack(g_ref)
    zero = jnp.zeros((BLOCK_LENGTH, PAIR), jnp.bfloat16)
    far = [jnp.where(valid_ref[first + i] > 0, ref[0], zero) for i, ref in enumerate(fetched)]
    keys = jnp.concatenate([k_ref[...]] + [f[:, :HEAD_WIDTH] for f in far], axis=0)
    values = jnp.concatenate([v_ref[...]] + [f[:, HEAD_WIDTH:] for f in far], axis=0)
    row = lax.broadcasted_iota(jnp.int32, (keys_n, rows_n), 1) % BLOCK_LENGTH + b * BLOCK_LENGTH
    key = lax.broadcasted_iota(jnp.int32, (keys_n, rows_n), 0)
    mask = (key < local) & (key <= row)
    for i in range(CHOSEN_BLOCKS):
        begin = local + i * BLOCK_LENGTH
        limit = jnp.where(valid_ref[first + i] > 0, begin + BLOCK_LENGTH, begin)
        mask = mask | ((key >= begin) & (key < limit))
    nt = (((1,), (1,)), ((), ()))
    tn = (((0,), (0,)), ((), ()))
    scores = lax.dot_general(keys, queries, nt, preferred_element_type=jnp.float32) * scale
    prob = jnp.where(mask, jnp.exp(scores - lse_ref[0, 0]), 0.0)
    dprob = lax.dot_general(values, grads, nt, preferred_element_type=jnp.float32)
    dscore = (prob * (dprob - delta_ref[0, 0])).astype(jnp.bfloat16)
    prob_low = prob.astype(jnp.bfloat16)
    dq = (lax.dot_general(dscore, keys, tn, preferred_element_type=jnp.float32) * scale).astype(
        jnp.bfloat16
    )
    for i in range(GROUP):
        dq_ref[:, i * HEAD_WIDTH : (i + 1) * HEAD_WIDTH] = dq[
            i * BLOCK_LENGTH : (i + 1) * BLOCK_LENGTH
        ]
    dk = jnp.dot(dscore, queries, preferred_element_type=jnp.float32) * scale
    dv = jnp.dot(prob_low, grads, preferred_element_type=jnp.float32)

    @pl.when(b == 0)
    def _():
        dk_ref[...] = dk[:local]
        dv_ref[...] = dv[:local]

    @pl.when(b > 0)
    def _():
        dk_ref[...] += dk[:local]
        dv_ref[...] += dv[:local]

    for i in range(CHOSEN_BLOCKS):
        at = pl.ds(local + i * BLOCK_LENGTH, BLOCK_LENGTH)
        lo = local + i * BLOCK_LENGTH

        @pl.when(valid_ref[first + i] > 0)
        def _():
            slot = place_ref[first + i]
            part_ref[slot, :, :HEAD_WIDTH] = dk[lo : lo + BLOCK_LENGTH].astype(jnp.bfloat16)
            part_ref[slot, :, HEAD_WIDTH:] = dv[lo : lo + BLOCK_LENGTH].astype(jnp.bfloat16)


def attend_call(slot_place, valid, queries, grads, keys, values, lse, delta, slots):
    slot_total = slots.shape[0]
    group_width = GROUP * HEAD_WIDTH

    def far_spec(i):
        return pl.BlockSpec(
            (1, BLOCK_LENGTH, PAIR),
            lambda h, b, sp, va: (sp[(b * KV_HEADS + h) * CHOSEN_BLOCKS + i], 0, 0),
        )

    rows = pl.BlockSpec((BLOCK_LENGTH, group_width), lambda h, b, sp, va: (b, h))
    shard = pl.BlockSpec((TOKENS, HEAD_WIDTH), lambda h, b, sp, va: (0, h))
    stat = pl.BlockSpec((1, 1, 1, GROUP * BLOCK_LENGTH), lambda h, b, sp, va: (b, h, 0, 0))
    return pl.pallas_call(
        attend_kernel,
        grid_spec=pltpu.PrefetchScalarGridSpec(
            num_scalar_prefetch=2,
            grid=(KV_HEADS, TOKENS // BLOCK_LENGTH),
            in_specs=[rows, rows, shard, shard, stat, stat, far_spec(0), far_spec(1), far_spec(2)],
            out_specs=[
                rows,
                shard,
                shard,
                pl.BlockSpec((slot_total, BLOCK_LENGTH, PAIR), lambda h, b, sp, va: (0, 0, 0)),
            ],
        ),
        out_shape=(
            jax.ShapeDtypeStruct(queries.shape, jnp.bfloat16),
            jax.ShapeDtypeStruct(keys.shape, jnp.float32),
            jax.ShapeDtypeStruct(keys.shape, jnp.float32),
            jax.ShapeDtypeStruct(slots.shape, jnp.bfloat16),
        ),
        compiler_params=pltpu.CompilerParams(vmem_limit_bytes=40 * 1024 * 1024),
        name="attend_blocks",
    )(slot_place, valid, queries, grads, keys, values, lse, delta, slots, slots, slots)


def request_table(choices, ring):
    number = choices.shape[0]
    active = choices >= 0
    owner = jnp.where(active, choices // 2, -1)
    position = jnp.arange(number, dtype=jnp.int32)
    same = (owner[:, None] == owner[None, :]) & active[None, :]
    same = same & (position[None, :] < position[:, None])
    rank = jnp.sum(same.astype(jnp.int32), axis=1)
    cls = owner // (2 * ring) * 2 + owner % 2
    slot = (cls * ring + owner // 2 % ring) * CAP + rank
    slot = jnp.where(active, slot, -1)
    unit = choices % 2 * KV_HEADS + position // CHOSEN_BLOCKS % KV_HEADS
    spot = jnp.arange(4 * ring * CAP, dtype=jnp.int32)
    match = slot[:, None] == spot[None, :]
    want = jnp.max(jnp.where(match, unit[:, None], -1), axis=0)
    want = want.reshape(4, 1, ring * CAP)
    want = jnp.pad(want, ((0, 0), (0, 7), (0, 128 - ring * CAP)), constant_values=-1)
    return jnp.maximum(slot, 0), active.astype(jnp.int32), want


def body(
    query_states,
    key_activations,
    value_activations,
    out_grad,
    logsumexp,
    row_delta,
    layer_input,
    chosen,
):
    shards = lax.axis_size("ctx")
    replicas = lax.axis_size("dp")
    ring = shards // 4
    slot_place, valid, want = request_table(chosen[0].reshape(-1), ring)
    keys, values = key_activations[0], value_activations[0]
    slots, wants = gather_call(ring, keys, values, want)

    def blockwise(stat):
        return (
            stat[0]
            .reshape(KV_HEADS, GROUP, 2, BLOCK_LENGTH)
            .transpose(2, 0, 1, 3)
            .reshape(2, KV_HEADS, 1, GROUP * BLOCK_LENGTH)
            .astype(jnp.float32)
        )

    query_grad, dk, dv, parts = attend_call(
        slot_place, valid, query_states[0], out_grad[0], keys, values,
        blockwise(logsumexp), blockwise(row_delta),
        slots.reshape(4 * ring * CAP, BLOCK_LENGTH, PAIR),
    )
    key_gradient, value_gradient = reduce_call(
        ring, parts.reshape(4, ring, CAP, BLOCK_LENGTH, PAIR), wants, dk, dv
    )
    weight_scale = 1.0 / math.sqrt(TOKENS * shards * replicas)
    key_weight_grad = lax.psum_scatter(
        jnp.einsum("td,tk->dk", layer_input[0], key_gradient, preferred_element_type=jnp.float32)
        * weight_scale,
        ("ctx", "dp"),
        scatter_dimension=0,
        tiled=True,
    )
    return (query_grad[None], key_gradient[None], value_gradient[None], key_weight_grad)


def solution(mesh):
    seq = P("dp", "ctx", None)
    stat = P("dp", None, "ctx")
    return jax.shard_map(
        body,
        mesh=mesh,
        in_specs=(seq, seq, seq, seq, stat, stat, seq, P("dp", "ctx", None, None)),
        out_specs=(seq, seq, seq, P(("ctx", "dp"), None)),
        check_vma=False,
    )
```

time: 1170 us -> 641 us (0.55)
  waiting for transfers between devices: 1040 us -> 486 us
  Pallas kernels: 0 us -> 127 us
  local copies, waits for them, and re-layouts: 62.8 us -> 9.72 us
  starting transfers between devices: 29.4 us -> 0.04 us
  other arithmetic: 13.8 us -> 0.32 us
  matrix products: 15.7 us -> 2.7 us
    all_to_all x3 -> x0, waiting for transfers between devices: 554 us -> none  [the longest x1 357 us: body(): lax.all_to_all(outgoing_back.reshape(shards, CAP, BLOCK_LENGTH, 2, HEAD_W...]
    pallas_call x0 -> x3, Pallas kernels: none -> 127 us  [the longest x1 62.3 us: gather_call(): pl.pallas_call(functools.partial(gather_kernel, ring), out_shape=(jax.Sha...]
    all_to_all x3 -> x0, starting transfers between devices: 29.2 us -> none  [the longest x1 17 us: body(): lax.all_to_all(slot_unit.reshape(shards, CAP), 'ctx', split_axis=0, conca...]
    gather x5 -> x0, local copies, waits for them, and re-layouts: 24.6 us -> none  [the longest x2 18.6 us: body(): jnp.take(partials, jnp.maximum(slot_request, 0), axis=0)]
    dot_general x12 -> x1, matrix products: 15.7 us -> 2.7 us  [body(): jnp.einsum('td,tk->dk', layer_input[0], key_gradient, preferred_element_t...]
    reshape x7 -> x1, local copies, waits for them, and re-layouts: 12.4 us -> 0.08 us  [request_table(): want = want.reshape(4, 1, ring * CAP)]
  transfers between devices with their start and end apart: 4 -> 1, of which waited for: 4 -> 1; matrix products, arithmetic and copies ran while one was open for 1% -> 0% of each run, Pallas kernels for 0% -> 0%
where the time goes in v1:
time: 641 us; the launch traced here: 640 us
  waiting for transfers between devices  486 us (76%)
  Pallas kernels  127 us (20%)
  between operations  14.1 us (2%)
  local copies, waits for them, and re-layouts  9.72 us (2%)
    unnamed x2, waiting for transfers between devices  486 us
    pallas_call x1, Pallas kernels, gather_call(): pl.pallas_call(functools.partial(gather_kernel, ring), out_shape=(jax.Sha...  62.3 us
    pallas_call x1, Pallas kernels, reduce_call(): pl.pallas_call(functools.partial(reduce_kernel, ring), out_shape=(jax.Sha...  58 us
  transfers between devices with their start and end apart: 1, of which 1 were waited for; matrix products, arithmetic and copies ran while one was open for 0% of the time, Pallas kernels for 0%

profile of v1, /device:TPU:24, one launch (start us, length us, event | category | flops | bytes accessed | tf_op | source)
XLA Modules:
  0.0 640.3 jit_solution(8668678956734368691)
XLA Ops:
  7.2 0.0 copy-start
  7.2 0.0 all-reduce.4.cloned.1.call-start
  7.2 0.8 copy.27
  8.1 0.1 reshape_squeeze.2
  8.2 0.2 convert_reduce_fusion
  8.4 0.1 select_reduce_fusion
  8.5 0.1 reshape.234
  8.6 0.8 reshape.239
  9.3 0.1 reshape.237.lse_ref
  9.4 0.8 reshape.240
  10.2 0.1 reshape.238.delta_ref
  10.3 0.0 copy-start.1
  10.3 0.9 copy-done.1
  11.2 0.0 copy-start.2
  11.2 0.9 copy-done.2
  12.1 62.3 %gather_blocks.1 = (bf16[4,16,2,64,256]{4,3,2,1,0:T(8,128)(2,1)S(1)}, s32[4,8,128]{2,1,0:T(8,128)S(1)}) custom-call(bf16[128,512]{1,0:T(8,128)(2,1)S(1)} %bitcast.28, bf16[128,512]{1,0:T(8,128)(2,1)S(1)} %bitcast.30, s32[4,8,128]{2,1,0:T(8,128)S(1)} %pad.4.want_ref), custom_call_target="tpu_custom_call" | custom-call | tf_op jit(solution)/shard_map/gather_blocks/pallas_call | solution.py:169
  74.4 0.0 copy-start.3
  74.4 1.0 copy-done.3
  75.5 0.0 copy-start.4
  75.5 1.0 copy-done.4
  76.5 7.1 %attend_blocks.1 = (bf16[128,2048]{1,0:T(8,128)(2,1)}, f32[128,512]{1,0:T(8,128)S(1)}, f32[128,512]{1,0:T(8,128)S(1)}, bf16[128,64,256]{2,1,0:T(8,128)(2,1)S(1)}) custom-call(s32[24]{0:T(128)S(1)} %get-tuple-element.36.place_ref, s32[24]{0:T(128)S(1)} %get-tuple-element.39.valid_ref, bf16[128,2048]{1,0:T(8,128)(2,1)S(1)} %bitcast.32, ...), custom_call_target="tpu_custom_call" | custom-call | tf_op jit(solution)/shard_map/attend_blocks/pallas_call | solution.py:431
  83.7 58.0 %reduce_blocks.1 = (bf16[128,512]{1,0:T(8,128)(2,1)S(1)}, bf16[128,512]{1,0:T(8,128)(2,1)S(1)}) custom-call(bf16[4,16,2,64,256]{4,3,2,1,0:T(8,128)(2,1)S(1)} %bitcast.27, s32[4,8,128]{2,1,0:T(8,128)S(1)} %get-tuple-element.15.wants_ref, f32[128,512]{1,0:T(8,128)S(1)} %get-tuple-element.16.dk_ref, f32[128,512]{1,0:T(8,128)S(1)} %get-tuple-element.17.dv_ref), custom_call_target="tpu_custom_call" | custom-call | tf_op jit(solution)/shard_map/reduce_blocks/pallas_call | solution.py:326
  141.6 0.0 copy-done
  141.7 2.7 multiply_bitcast_fusion
  144.4 0.0 all-reduce.4.cloned.1.call-update
  144.4 485.9 %all-reduce.4.cloned.1.call-done = f32[2048,512]{0,1:T(8,128)} async-done(((f32[2048,512]{0,1:T(8,128)}), f32[2048,512]{0,1:T(8,128)}) %all-reduce.4.cloned.1.call-update) | async-done | bytes 4194320
  630.3 1.1 constant_dynamic-slice_fusion
  631.4 0.7 copy.31
  632.1 0.7 copy.41
  632.8 0.7 copy.42
  (6 shorter events, 0.1 us)
Async XLA Ops:
  7.2 134.5 %copy-start = (bf16[1,128,2048]{2,1,0:T(8,128)(2,1)S(1)}, bf16[1,128,2048]{2,1,0:T(8,128)(2,1)}, u32[]{:S(2)}) copy-start(bf16[1,128,2048]{2,1,0:T(8,128)(2,1)} %param.14) | copy-start | bytes 1572868
  7.2 623.1 %all-reduce.4.cloned.1.call-start = ((), (), s32[]{:S(2)}) async-start(), calls=%async_computation | async-start | bytes 8388608
  10.3 0.9 copy-start.1
  11.2 0.9 copy-start.2
  74.4 1.0 copy-start.3
  75.5 1.0 copy-start.4
Sparse Core Ops, SparseCore 0:
  144.5 485.7 all-reduce.3

commit v2 on v1

--- a/solution.py
+++ b/solution.py
@@ -37,30 +37,50 @@
     return x * (2 * ring) + lax.rem(z + step + ring, ring) * 2 + c
 
 
-def greet(ring):
+def column_mate(step):
+    i, d = lax.axis_index("ctx"), lax.axis_index("dp")
+    rows = lax.axis_size("dp") // 2
+    return {"ctx": i, "dp": lax.rem(d // 2 + step, rows) * 2 + lax.rem(d, 2)}
+
+
+def row_mate(ring, j):
+    x, z, c = place(ring)
+    d = lax.axis_index("dp")
+    lo, hi = lax.rem(x + j // 2, 2), lax.rem(lax.rem(d, 2) + j % 2, 2)
+    return {"ctx": lo * (2 * ring) + z * 2 + c, "dp": d // 2 * 2 + hi}, lo, hi
+
+
+def greet(others):
     barrier = pltpu.get_barrier_semaphore()
-    for other in (along(ring, 1), along(ring, -1)) + tuple(member(ring, j)[0] for j in (1, 2, 3)):
-        pl.semaphore_signal(barrier, inc=1, device_id={"ctx": other}, device_id_type=MESH)
-    pl.semaphore_wait(barrier, 5)
+    for other in others:
+        pl.semaphore_signal(barrier, inc=1, device_id=other, device_id_type=MESH)
+    pl.semaphore_wait(barrier, len(others))
+
+
+def neighbours(ring):
+    places = [along(ring, 1), along(ring, -1)] + [member(ring, j)[0] for j in (1, 2, 3)]
+    return [{"ctx": other} for other in places]
 
 
 def push(src, dst, send, recv, other):
+    other = other if isinstance(other, dict) else {"ctx": other}
     return pltpu.make_async_remote_copy(
         src_ref=src, dst_ref=dst, send_sem=send, recv_sem=recv,
-        device_id={"ctx": other}, device_id_type=MESH,
+        device_id=other, device_id_type=MESH,
     )
 
 
 def gather_kernel(
-    ring, k_ref, v_ref, want_ref, slots_ref, wants_ref,
-    up, down, stage, work, want_smem,
+    ring, rows_y, k_ref, v_ref, want_ref, x_ref, slots_ref, wants_ref, xg_ref,
+    up, down, stage, work, want_smem, xt,
     up_send, up_recv, down_send, down_recv, w_send, w_recv, s_send, s_recv, local_sem, smem_sem,
+    x_send, x_recv,
 ):
     half = ring // 2
     x, z, c = place(ring)
     cls = x * 2 + c
     above, below = along(ring, 1), along(ring, -1)
-    greet(ring)
+    greet(neighbours(ring) + [column_mate(t) for t in range(1, rows_y)])
 
     def up_copy(s, part, src=None):
         src = up.at[s - 1, part] if src is None else src
@@ -118,6 +138,41 @@
 
     extract(0, k_ref, v_ref)
 
+    y = lax.axis_index("dp") // 2
+    lines = 16 * ring
+    half_width = lines * rows_y
+
+    def x_copy(t):
+        return push(
+            xt.at[t], xg_ref.at[:, :, pl.ds(pl.multiple_of(y * TOKENS, TOKENS), TOKENS)],
+            x_send.at[t], x_recv.at[t], column_mate(t),
+        )
+
+    def keep_copy():
+        return pltpu.make_async_copy(
+            xt.at[0], xg_ref.at[:, :, pl.ds(pl.multiple_of(y * TOKENS, TOKENS), TOKENS)], x_send.at[0]
+        )
+
+    def deal(t):
+        to = lax.rem(y + t, rows_y)
+        line = lax.broadcasted_iota(jnp.int32, (lines, half_width), 0)
+        column = lax.broadcasted_iota(jnp.int32, (lines, half_width), 1)
+        core, high, spot = line // (8 * ring), line // (4 * ring) % 2, line % (4 * ring)
+        source = spot // 4 * (16 * rows_y) + core * (8 * rows_y) + to * 8 + high * 4 + spot % 4
+        pick = jnp.where(column == source, 1.0, 0.0).astype(jnp.bfloat16)
+        for lo in range(2):
+            part = x_ref[:, lo * half_width : (lo + 1) * half_width]
+            xt[t, lo] = lax.dot_general(
+                pick, part, (((1,), (1,)), ((), ())), preferred_element_type=jnp.float32
+            ).astype(jnp.bfloat16)
+
+    for t in range(rows_y):
+        deal(t)
+        if t == 0:
+            keep_copy().start()
+        else:
+            x_copy(t).start()
+
     def step(s, _):
         for part in range(2):
             up_copy(s, part, k_ref).wait_recv()
@@ -160,26 +215,36 @@
         return 0
 
     lax.fori_loop(0, ring, drain_slots, 0)
-
-
-def gather_call(ring, keys, values, want):
+    keep_copy().wait()
+    for t in range(1, rows_y):
+        x_copy(t).wait()
+
+
+def gather_call(ring, rows_y, keys, values, want, inputs):
     half = ring // 2
+    lines = 16 * ring
     ring_buffer = pltpu.VMEM((half, 2, TOKENS, KV_HEADS * HEAD_WIDTH), jnp.bfloat16)
     ring_sem = pltpu.SemaphoreType.DMA((half, 2))
     return pl.pallas_call(
-        functools.partial(gather_kernel, ring),
+        functools.partial(gather_kernel, ring, rows_y),
         out_shape=(
             jax.ShapeDtypeStruct((4, ring, CAP, BLOCK_LENGTH, PAIR), jnp.bfloat16),
             jax.ShapeDtypeStruct((4, 8, 128), jnp.int32),
+            jax.ShapeDtypeStruct((2, lines, rows_y * TOKENS), jnp.bfloat16),
         ),
-        in_specs=[pl.BlockSpec(memory_space=pltpu.VMEM)] * 3,
-        out_specs=(pl.BlockSpec(memory_space=pl.ANY), pl.BlockSpec(memory_space=pltpu.VMEM)),
+        in_specs=[pl.BlockSpec(memory_space=pltpu.VMEM)] * 4,
+        out_specs=(
+            pl.BlockSpec(memory_space=pl.ANY),
+            pl.BlockSpec(memory_space=pltpu.VMEM),
+            pl.BlockSpec(memory_space=pltpu.VMEM),
+        ),
         scratch_shapes=[
             ring_buffer,
             ring_buffer,
             pltpu.VMEM((ring, 4, CAP, BLOCK_LENGTH, PAIR), jnp.bfloat16),
             pltpu.VMEM((UNITS, BLOCK_LENGTH, PAIR), jnp.bfloat16),
             pltpu.SMEM((4, 8, 128), jnp.int32),
+            pltpu.VMEM((rows_y, 2, lines, TOKENS), jnp.bfloat16),
             ring_sem, ring_sem, ring_sem, ring_sem,
             pltpu.SemaphoreType.DMA((3,)),
             pltpu.SemaphoreType.DMA((3,)),
@@ -187,161 +252,271 @@
             pltpu.SemaphoreType.DMA((3, ring)),
             pltpu.SemaphoreType.DMA((ring,)),
             pltpu.SemaphoreType.DMA,
+            pltpu.SemaphoreType.DMA((rows_y,)),
+            pltpu.SemaphoreType.DMA((rows_y,)),
         ],
         compiler_params=pltpu.CompilerParams(
             collective_id=0, has_side_effects=True, vmem_limit_bytes=40 * 1024 * 1024
         ),
         name="gather_blocks",
-    )(keys, values, want)
+    )(keys, values, want, inputs)
 
 
 def reduce_kernel(
-    ring, part_ref, wants_ref, dk_ref, dv_ref, kg_ref, vg_ref,
-    up, down, ups, downs, arrived, want_smem,
+    ring, rows_y, weight_scale,
+    part_ref, wants_ref, dk_ref, dv_ref, xg_ref, kg_ref, vg_ref, wg_ref,
+    up, down, ups, downs, arrived, want_smem, all_k, own, across, shared, from_x, pieces, from_z,
     up_send, up_recv, down_send, down_recv, s_send, s_recv, smem_sem,
+    y_send, y_recv, c_send, c_recv, x_send, x_recv, z_send, z_recv,
 ):
     half = ring // 2
     x, z, c = place(ring)
+    high = lax.rem(lax.axis_index("dp"), 2)
     cls = x * 2 + c
     above, below = along(ring, 1), along(ring, -1)
-    greet(ring)
-
-    def slot_copy(j, r):
+    far_x = [row_mate(ring, j)[0] for j in (1, 3)]
+    far_z = [{"ctx": along(ring, d)} for d in range(2, ring - 1)]
+    greet(neighbours(ring) + [column_mate(t) for t in range(1, rows_y)] + far_x + far_z)
+
+    def slot_copy(part, j, r):
         other, other_cls = member(ring, j)
         owner = lax.rem(z + r, ring)
         return push(
-            part_ref.at[other_cls, owner], arrived.at[j - 1, r],
-            s_send.at[j - 1, r], s_recv.at[j - 1, r], other,
-        )
-
-    for j in (1, 2, 3):
-        slot_copy(j, half).start()
-
-    def send_slots(s, _):
+            part_ref.at[part, other_cls, owner], arrived.at[part, j - 1, r],
+            s_send.at[part, j - 1, r], s_recv.at[part, j - 1, r], other,
+        )
+
+    def send_slots(part):
         for j in (1, 2, 3):
-            slot_copy(j, half - s).start()
-            slot_copy(j, half + s).start()
-        return 0
-
-    lax.fori_loop(1, half, send_slots, 0)
-    for j in (1, 2, 3):
-        slot_copy(j, 0).start()
+            slot_copy(part, j, half).start()
+
+        def some(s, _):
+            for j in (1, 2, 3):
+                slot_copy(part, j, half - s).start()
+                slot_copy(part, j, half + s).start()
+            return 0
+
+        lax.fori_loop(1, half, some, 0)
+        for j in (1, 2, 3):
+            slot_copy(part, j, 0).start()
+
+    send_slots(0)
     table = pltpu.make_async_copy(wants_ref, want_smem, smem_sem)
     table.start()
-    blank = jnp.zeros((TOKENS, KV_HEADS * HEAD_WIDTH), jnp.bfloat16)
-    up[0, 1] = blank
-    down[0, 0] = blank
+    blank = jnp.zeros((BLOCK_LENGTH, KV_HEADS * HEAD_WIDTH), jnp.bfloat16)
+    for part in range(2):
+        up[part, 0, 1] = blank
+        down[part, 0, 0] = blank
     table.wait()
 
-    def up_copy(s, part):
-        return push(ups.at[s, part], up.at[s, part], up_send.at[s, part], up_recv.at[s, part], above)
-
-    def down_copy(s, part):
+    def up_copy(part, s, b):
         return push(
-            downs.at[s, part], down.at[s, part], down_send.at[s, part], down_recv.at[s, part], below
-        )
-
-    def total(r, part, incoming, target):
+            ups.at[part, s, b], up.at[part, s, b], up_send.at[part, s, b], up_recv.at[part, s, b], above
+        )
+
+    def down_copy(part, s, b):
+        return push(
+            downs.at[part, s, b], down.at[part, s, b],
+            down_send.at[part, s, b], down_recv.at[part, s, b], below,
+        )
+
+    def total(part, r, b, incoming, targets):
         owner = lax.rem(z + r, ring)
-        lanes = pl.ds(part * HEAD_WIDTH, HEAD_WIDTH)
         units = [[want_smem[j, 0, owner * CAP + rank] for rank in range(CAP)] for j in range(4)]
+        for h in range(KV_HEADS):
+            lanes = slice(h * HEAD_WIDTH, (h + 1) * HEAD_WIDTH)
+            acc = jnp.zeros((BLOCK_LENGTH, HEAD_WIDTH), jnp.float32)
+            for ref in incoming:
+                acc = acc + ref[:, lanes].astype(jnp.float32)
+            for j in range(4):
+                for rank in range(CAP):
+                    if j == 0:
+                        term = part_ref[part, cls, owner, rank]
+                    else:
+                        term = arrived[part, j - 1, r, rank]
+                    hit = units[j][rank] == b * KV_HEADS + h
+                    acc = acc + jnp.where(hit, term.astype(jnp.float32), 0.0)
+            for target in targets:
+                target[:, lanes] = acc.astype(jnp.bfloat16)
+
+    def phase(part, hooks, after):
+        for j in (1, 2, 3):
+            slot_copy(part, j, half).wait_recv()
+        total(part, half, 0, [], [ups.at[part, 0, 0]])
+        up_copy(part, 0, 0).start()
+        total(part, half, 1, [], [downs.at[part, 0, 1]])
+        down_copy(part, 0, 1).start()
+
+        def step(s, _):
+            for j in (1, 2, 3):
+                slot_copy(part, j, half - s).wait_recv()
+                slot_copy(part, j, half + s).wait_recv()
+            up_copy(part, s - 1, 0).wait_recv()
+            total(part, half - s, 0, [up.at[part, s - 1, 0]], [ups.at[part, s, 0]])
+            up_copy(part, s, 0).start()
+            down_copy(part, s - 1, 1).wait_recv()
+            total(part, half + s, 1, [down.at[part, s - 1, 1]], [downs.at[part, s, 1]])
+            down_copy(part, s, 1).start()
+
+            @pl.when(s > 1)
+            def _():
+                up_copy(part, s - 1, 1).wait_recv()
+                down_copy(part, s - 1, 0).wait_recv()
+
+            total(part, half - s, 1, [up.at[part, s - 1, 1]], [ups.at[part, s, 1]])
+            up_copy(part, s, 1).start()
+            total(part, half + s, 0, [down.at[part, s - 1, 0]], [downs.at[part, s, 0]])
+            down_copy(part, s, 0).start()
+            for at, hook in hooks.items():
+                pl.when(s == at)(hook)
+            return 0
+
+        lax.fori_loop(1, half, step, 0)
+        for j in (1, 2, 3):
+            slot_copy(part, j, 0).wait_recv()
+        near, outs = ((dk_ref, (kg_ref, own)), (dv_ref, (vg_ref,)))[part]
         for b in range(2):
-            for h in range(KV_HEADS):
-                at = (pl.ds(b * BLOCK_LENGTH, BLOCK_LENGTH), pl.ds(h * HEAD_WIDTH, HEAD_WIDTH))
-                acc = jnp.zeros((BLOCK_LENGTH, HEAD_WIDTH), jnp.float32)
-                for ref in incoming:
-                    acc = acc + ref[at].astype(jnp.float32)
-                for j in range(4):
-                    for rank in range(CAP):
-                        if j == 0:
-                            term = part_ref[cls, owner, rank, :, lanes]
-                        else:
-                            term = arrived[j - 1, r, rank, :, lanes]
-                        hit = units[j][rank] == b * KV_HEADS + h
-                        acc = acc + jnp.where(hit, term.astype(jnp.float32), 0.0)
-                target[at] = acc.astype(jnp.bfloat16)
-
-    for j in (1, 2, 3):
-        slot_copy(j, half).wait_recv()
-    total(half, 0, [], ups.at[0, 0])
-    up_copy(0, 0).start()
-    total(half, 1, [], downs.at[0, 1])
-    down_copy(0, 1).start()
-
-    def step(s, _):
+            up_copy(part, half - 1, b).wait_recv()
+            down_copy(part, half - 1, b).wait_recv()
+            rows = pl.ds(b * BLOCK_LENGTH, BLOCK_LENGTH)
+            total(
+                part, 0, b,
+                [near.at[rows], up.at[part, half - 1, b], down.at[part, half - 1, b]],
+                [out.at[rows] for out in outs],
+            )
+        after()
+
+    y = lax.axis_index("dp") // 2
+
+    def y_copy(t):
+        return push(own, all_k.at[y], y_send.at[t - 1], y_recv.at[t - 1], column_mate(t))
+
+    def c_copy():
+        return push(across.at[:, 1 - c], shared, c_send, c_recv, member(ring, 1)[0])
+
+    def x_copy(j):
+        mate, lo, hi = row_mate(ring, j)
+        return push(
+            across.at[lo, c, hi], from_x.at[j - 1], x_send.at[j - 1], x_recv.at[j - 1], mate
+        )
+
+    def z_copy(d):
+        return push(
+            pieces.at[lax.rem(z + d, ring)], from_z.at[d - 1],
+            z_send.at[d - 1], z_recv.at[d - 1], along(ring, d),
+        )
+
+    def start_weights():
+        for t in range(1, rows_y):
+            y_copy(t).start()
+        all_k[y] = own[...]
+        send_slots(1)
+
+    def multiply():
+        for t in range(1, rows_y):
+            y_copy(t).wait_recv()
+        gathered = all_k[...].reshape(rows_y * TOKENS, KV_HEADS * HEAD_WIDTH)
+        for lo in range(2):
+            product = jnp.dot(xg_ref[lo], gathered, preferred_element_type=jnp.float32)
+            for core in range(2):
+                for hi in range(2):
+                    begin = (core * 2 + hi) * 4 * ring
+                    across[lo, core, hi] = product[begin : begin + 4 * ring]
+        c_copy().start()
+
+    def add_core():
+        c_copy().wait()
+        for lo in range(2):
+            for hi in range(2):
+                across[lo, c, hi] += shared[lo, hi]
         for j in (1, 2, 3):
-            slot_copy(j, half - s).wait_recv()
-            slot_copy(j, half + s).wait_recv()
-
-        up_copy(s - 1, 0).wait_recv()
-        total(half - s, 0, [up.at[s - 1, 0]], ups.at[s, 0])
-        up_copy(s, 0).start()
-        down_copy(s - 1, 1).wait_recv()
-        total(half + s, 1, [down.at[s - 1, 1]], downs.at[s, 1])
-        down_copy(s, 1).start()
-
-        @pl.when(s > 1)
-        def _():
-            up_copy(s - 1, 1).wait_recv()
-            down_copy(s - 1, 0).wait_recv()
-
-        total(half - s, 1, [up.at[s - 1, 1]], ups.at[s, 1])
-        up_copy(s, 1).start()
-        total(half + s, 0, [down.at[s - 1, 0]], downs.at[s, 0])
-        down_copy(s, 0).start()
-        return 0
-
-    lax.fori_loop(1, half, step, 0)
-    for j in (1, 2, 3):
-        slot_copy(j, 0).wait_recv()
-    for part, near, out in ((0, dk_ref, kg_ref), (1, dv_ref, vg_ref)):
-        up_copy(half - 1, part).wait_recv()
-        down_copy(half - 1, part).wait_recv()
-        total(0, part, [near, up.at[half - 1, part], down.at[half - 1, part]], out)
-
-    up_copy(0, 0).wait_send()
-    down_copy(0, 1).wait_send()
-
-    def drain(s, _):
-        for part in range(2):
-            up_copy(s, part).wait_send()
-            down_copy(s, part).wait_send()
-        return 0
-
-    lax.fori_loop(1, half, drain, 0)
-
-    def drain_slots(r, _):
+            x_copy(j).start()
+
+    def add_row():
         for j in (1, 2, 3):
-            slot_copy(j, r).wait_send()
-        return 0
-
-    lax.fori_loop(0, ring, drain_slots, 0)
-
-
-def reduce_call(ring, parts, wants, dk, dv):
+            x_copy(j).wait()
+        value = across[x, c, high] + from_x[0] + from_x[1] + from_x[2]
+        for i in range(ring):
+            pieces[i] = value[4 * i : 4 * i + 4]
+        for d in range(1, ring):
+            z_copy(d).start()
+
+    def nothing():
+        pass
+
+    phase(0, {}, start_weights)
+    hooks = {2: multiply, 4: add_core, 6: add_row} if half >= 8 else {}
+    phase(1, hooks, nothing)
+    if not hooks:
+        multiply()
+        add_core()
+        add_row()
+    value = pieces[z]
+    for d in range(1, ring):
+        z_copy(d).wait_recv()
+        value = value + from_z[d - 1]
+    wg_ref[...] = value * weight_scale
+
+    for t in range(1, rows_y):
+        y_copy(t).wait_send()
+    for d in range(1, ring):
+        z_copy(d).wait_send()
+    for part in range(2):
+        up_copy(part, 0, 0).wait_send()
+        down_copy(part, 0, 1).wait_send()
+
+        def drain(s, _):
+            for b in range(2):
+                up_copy(part, s, b).wait_send()
+                down_copy(part, s, b).wait_send()
+            return 0
+
+        lax.fori_loop(1, half, drain, 0)
+
+        def drain_slots(r, _):
+            for j in (1, 2, 3):
+                slot_copy(part, j, r).wait_send()
+            return 0
+
+        lax.fori_loop(0, ring, drain_slots, 0)
+
+
+def reduce_call(ring, rows_y, weight_scale, parts, wants, dk, dv, xg):
     half = ring // 2
     width = KV_HEADS * HEAD_WIDTH
-    ring_buffer = pltpu.VMEM((half, 2, TOKENS, width), jnp.bfloat16)
-    ring_sem = pltpu.SemaphoreType.DMA((half, 2))
+    ring_buffer = pltpu.VMEM((2, half, 2, BLOCK_LENGTH, width), jnp.bfloat16)
+    ring_sem = pltpu.SemaphoreType.DMA((2, half, 2))
+    dma = pltpu.SemaphoreType.DMA
     return pl.pallas_call(
-        functools.partial(reduce_kernel, ring),
-        out_shape=(jax.ShapeDtypeStruct((TOKENS, width), jnp.bfloat16),) * 2,
-        in_specs=[pl.BlockSpec(memory_space=pltpu.VMEM)] * 4,
-        out_specs=(pl.BlockSpec(memory_space=pltpu.VMEM),) * 2,
+        functools.partial(reduce_kernel, ring, rows_y, weight_scale),
+        out_shape=(
+            jax.ShapeDtypeStruct((TOKENS, width), jnp.bfloat16),
+            jax.ShapeDtypeStruct((TOKENS, width), jnp.bfloat16),
+            jax.ShapeDtypeStruct((4, width), jnp.float32),
+        ),
+        in_specs=[pl.BlockSpec(memory_space=pltpu.VMEM)] * 5,
+        out_specs=(pl.BlockSpec(memory_space=pltpu.VMEM),) * 3,
         scratch_shapes=[
             ring_buffer, ring_buffer, ring_buffer, ring_buffer,
-            pltpu.VMEM((3, ring, CAP, BLOCK_LENGTH, PAIR), jnp.bfloat16),
+            pltpu.VMEM((2, 3, ring, CAP, BLOCK_LENGTH, HEAD_WIDTH), jnp.bfloat16),
             pltpu.SMEM((4, 8, 128), jnp.int32),
+            pltpu.VMEM((rows_y, TOKENS, width), jnp.bfloat16),
+            pltpu.VMEM((TOKENS, width), jnp.bfloat16),
+            pltpu.VMEM((2, 2, 2, 4 * ring, width), jnp.float32),
+            pltpu.VMEM((2, 2, 4 * ring, width), jnp.float32),
+            pltpu.VMEM((3, 4 * ring, width), jnp.float32),
+            pltpu.VMEM((ring, 4, width), jnp.float32),
+            pltpu.VMEM((ring - 1, 4, width), jnp.float32),
             ring_sem, ring_sem, ring_sem, ring_sem,
-            pltpu.SemaphoreType.DMA((3, ring)),
-            pltpu.SemaphoreType.DMA((3, ring)),
-            pltpu.SemaphoreType.DMA,
+            dma((2, 3, ring)), dma((2, 3, ring)), dma,
+            dma((rows_y - 1,)), dma((rows_y - 1,)), dma, dma,
+            dma((3,)), dma((3,)), dma((ring - 1,)), dma((ring - 1,)),
         ],
         compiler_params=pltpu.CompilerParams(
-            collective_id=1, has_side_effects=True, vmem_limit_bytes=40 * 1024 * 1024
+            collective_id=1, has_side_effects=True, vmem_limit_bytes=48 * 1024 * 1024
         ),
         name="reduce_blocks",
-    )(parts, wants, dk, dv)
+    )(parts, wants, dk, dv, xg)
 
 
 def attend_kernel(
@@ -405,14 +580,13 @@
         dv_ref[...] += dv[:local]
 
     for i in range(CHOSEN_BLOCKS):
-        at = pl.ds(local + i * BLOCK_LENGTH, BLOCK_LENGTH)
         lo = local + i * BLOCK_LENGTH
 
         @pl.when(valid_ref[first + i] > 0)
         def _():
             slot = place_ref[first + i]
-            part_ref[slot, :, :HEAD_WIDTH] = dk[lo : lo + BLOCK_LENGTH].astype(jnp.bfloat16)
-            part_ref[slot, :, HEAD_WIDTH:] = dv[lo : lo + BLOCK_LENGTH].astype(jnp.bfloat16)
+            part_ref[0, slot] = dk[lo : lo + BLOCK_LENGTH].astype(jnp.bfloat16)
+            part_ref[1, slot] = dv[lo : lo + BLOCK_LENGTH].astype(jnp.bfloat16)
 
 
 def attend_call(slot_place, valid, queries, grads, keys, values, lse, delta, slots):
@@ -438,14 +612,16 @@
                 rows,
                 shard,
                 shard,
-                pl.BlockSpec((slot_total, BLOCK_LENGTH, PAIR), lambda h, b, sp, va: (0, 0, 0)),
+                pl.BlockSpec(
+                    (2, slot_total, BLOCK_LENGTH, HEAD_WIDTH), lambda h, b, sp, va: (0, 0, 0, 0)
+                ),
             ],
         ),
         out_shape=(
             jax.ShapeDtypeStruct(queries.shape, jnp.bfloat16),
             jax.ShapeDtypeStruct(keys.shape, jnp.float32),
             jax.ShapeDtypeStruct(keys.shape, jnp.float32),
-            jax.ShapeDtypeStruct(slots.shape, jnp.bfloat16),
+            jax.ShapeDtypeStruct((2, slot_total, BLOCK_LENGTH, HEAD_WIDTH), jnp.bfloat16),
         ),
         compiler_params=pltpu.CompilerParams(vmem_limit_bytes=40 * 1024 * 1024),
         name="attend_blocks",
@@ -487,7 +663,8 @@
     ring = shards // 4
     slot_place, valid, want = request_table(chosen[0].reshape(-1), ring)
     keys, values = key_activations[0], value_activations[0]
-    slots, wants = gather_call(ring, keys, values, want)
+    rows_y = replicas // 2
+    slots, wants, xg = gather_call(ring, rows_y, keys, values, want, layer_input[0])
 
     def blockwise(stat):
         return (
@@ -503,16 +680,10 @@
         blockwise(logsumexp), blockwise(row_delta),
         slots.reshape(4 * ring * CAP, BLOCK_LENGTH, PAIR),
     )
-    key_gradient, value_gradient = reduce_call(
-        ring, parts.reshape(4, ring, CAP, BLOCK_LENGTH, PAIR), wants, dk, dv
-    )
     weight_scale = 1.0 / math.sqrt(TOKENS * shards * replicas)
-    key_weight_grad = lax.psum_scatter(
-        jnp.einsum("td,tk->dk", layer_input[0], key_gradient, preferred_element_type=jnp.float32)
-        * weight_scale,
-        ("ctx", "dp"),
-        scatter_dimension=0,
-        tiled=True,
+    key_gradient, value_gradient, key_weight_grad = reduce_call(
+        ring, rows_y, weight_scale,
+        parts.reshape(2, 4, ring, CAP, BLOCK_LENGTH, HEAD_WIDTH), wants, dk, dv, xg,
     )
     return (query_grad[None], key_gradient[None], value_gradient[None], key_weight_grad)
 

time: 641 us -> 173 us (0.27)
  waiting for transfers between devices: 486 us -> 0 us
  Pallas kernels: 127 us -> 161 us
  between operations: 14.1 us -> 0.68 us
    unnamed x2 -> x0, waiting for transfers between devices: 486 us -> none
    pallas_call x2, Pallas kernels: 120 us -> 153 us  [the longest x1 90.9 us: reduce_call(): pl.pallas_call(functools.partial(reduce_kernel, ring, rows_y, weight_scal...]
  transfers between devices with their start and end apart: 1 -> 0, of which waited for: 1 -> 0; matrix products, arithmetic and copies ran while one was open for 0% -> 0% of each run, Pallas kernels for 0% -> 0%
where the time goes in v2:
time: 173 us; the launch traced here: 171 us
  Pallas kernels  161 us (93%)
  local copies, waits for them, and re-layouts  9.53 us (6%)
    pallas_call x1, Pallas kernels, reduce_call(): pl.pallas_call(functools.partial(reduce_kernel, ring, rows_y, weight_scal...  90.9 us
    pallas_call x1, Pallas kernels, gather_call(): pl.pallas_call(functools.partial(gather_kernel, ring, rows_y), out_shape=...  62.6 us
    unnamed x14, local copies, waits for them, and re-layouts  7.61 us
    pallas_call x1, Pallas kernels, attend_call(): pl.pallas_call(attend_kernel, grid_spec=pltpu.PrefetchScalarGridSpec(num_...  7.4 us

profile of v2, /device:TPU:24, one launch (start us, length us, event | category | flops | bytes accessed | tf_op | source)
XLA Modules:
  0.0 171.4 jit_solution(13895681198322822892)
XLA Ops:
  0.6 0.8 copy.20
  1.4 0.1 reshape_squeeze.2
  1.5 0.2 convert_reduce_fusion
  1.7 0.1 select_reduce_fusion
  1.8 0.1 reshape.234
  1.9 0.8 reshape.239
  2.7 0.1 reshape.237.lse_ref
  2.8 0.8 reshape.240
  3.6 0.1 reshape.238.delta_ref
  3.7 0.0 copy-start
  3.7 0.9 copy-done
  4.6 0.0 copy-start.1
  4.6 0.9 copy-done.1
  5.5 0.0 copy-start.4
  5.5 1.0 copy-done.4
  6.5 62.6 %gather_blocks.1 = (bf16[4,16,2,64,256]{4,3,2,1,0:T(8,128)(2,1)S(1)}, s32[4,8,128]{2,1,0:T(8,128)S(1)}, bf16[2,256,512]{2,1,0:T(8,128)(2,1)S(1)}) custom-call(bf16[128,512]{1,0:T(8,128)(2,1)S(1)} %bitcast.21, bf16[128,512]{1,0:T(8,128)(2,1)S(1)} %bitcast.23, s32[4,8,128]{2,1,0:T(8,128)S(1)} %pad.4.want_ref, bf16[128,2048]{1,0:T(8,128)(2,1)S(1)} %bitcast.27), custom_call_target="tpu_custom_call" | custom-call | tf_op jit(solution)/shard_map/gather_blocks/pallas_call | solution.py:228
  69.1 0.0 copy-start.2
  69.1 1.0 copy-done.2
  70.1 0.0 copy-start.3
  70.2 1.0 copy-done.3
  71.2 7.4 %attend_blocks.1 = (bf16[128,2048]{1,0:T(8,128)(2,1)}, f32[128,512]{1,0:T(8,128)S(1)}, f32[128,512]{1,0:T(8,128)S(1)}, bf16[2,128,64,128]{3,2,1,0:T(8,128)(2,1)S(1)}) custom-call(s32[24]{0:T(128)S(1)} %get-tuple-element.24.place_ref, s32[24]{0:T(128)S(1)} %get-tuple-element.27.valid_ref, bf16[128,2048]{1,0:T(8,128)(2,1)S(1)} %bitcast.25, ...), custom_call_target="tpu_custom_call" | custom-call | tf_op jit(solution)/shard_map/attend_blocks/pallas_call | solution.py:605
  78.6 90.9 %reduce_blocks.1 = (bf16[128,512]{1,0:T(8,128)(2,1)S(1)}, bf16[128,512]{1,0:T(8,128)(2,1)S(1)}, f32[4,512]{1,0:T(4,128)S(1)}) custom-call(bf16[2,4,16,2,64,128]{5,4,3,2,1,0:T(8,128)(2,1)S(1)} %bitcast.20, s32[4,8,128]{2,1,0:T(8,128)S(1)} %get-tuple-element.17.wants_ref, f32[128,512]{1,0:T(8,128)S(1)} %get-tuple-element.18.dk_ref, ...), custom_call_target="tpu_custom_call" | custom-call | tf_op jit(solution)/shard_map/reduce_blocks/pallas_call | solution.py:490
  169.5 0.7 copy.31
  170.1 0.7 copy.32
  170.8 0.6 copy.33
  (6 shorter events, 0.1 us)
Async XLA Ops:
  3.7 0.9 copy-start
  4.6 0.9 copy-start.1
  5.5 1.0 copy-start.4
  69.1 1.0 copy-start.2
  70.1 1.0 copy-start.3

commit v3 on v2

v3 whole, which is shorter than its diff:
```python
import functools
import math

import jax
import jax.numpy as jnp
from jax import lax
from jax.experimental import pallas as pl
from jax.experimental.pallas import tpu as pltpu
from jax.sharding import PartitionSpec as P

HEAD_WIDTH = 128
BLOCK_LENGTH = 64
CHOSEN_BLOCKS = 3
CAP = 2
KV_HEADS = 4
GROUP = 4
TOKENS = 128
UNITS = TOKENS // BLOCK_LENGTH * KV_HEADS
PAIR = 2 * HEAD_WIDTH
LAG = 4
AHEAD = 3
VMEM_BYTES = 58 * 1024 * 1024
MESH = pl.DeviceIdType.MESH


def place(ring):
    i = lax.axis_index("ctx")
    return i // (2 * ring), lax.rem(i // 2, ring), lax.rem(i, 2)


def member(ring, j):
    x, z, c = place(ring)
    mx = lax.rem(x + j // 2, 2)
    mc = lax.rem(c + j % 2, 2)
    return mx * (2 * ring) + z * 2 + mc, mx * 2 + mc


def along(ring, step):
    x, z, c = place(ring)
    return x * (2 * ring) + lax.rem(z + step + ring, ring) * 2 + c


def column_mate(step):
    i, d = lax.axis_index("ctx"), lax.axis_index("dp")
    rows = lax.axis_size("dp") // 2
    return {"ctx": i, "dp": lax.rem(d // 2 + step, rows) * 2 + lax.rem(d, 2)}


def row_mate(ring, j):
    x, z, c = place(ring)
    d = lax.axis_index("dp")
    lo, hi = lax.rem(x + j // 2, 2), lax.rem(lax.rem(d, 2) + j % 2, 2)
    return {"ctx": lo * (2 * ring) + z * 2 + c, "dp": d // 2 * 2 + hi}, lo, hi


def greet(others):
    barrier = pltpu.get_barrier_semaphore()
    for other in others:
        pl.semaphore_signal(barrier, inc=1, device_id=other, device_id_type=MESH)
    pl.semaphore_wait(barrier, len(others))


def neighbours(ring):
    places = [along(ring, 1), along(ring, -1)] + [member(ring, j)[0] for j in (1, 2, 3)]
    return [{"ctx": other} for other in places]


def push(src, dst, send, recv, other):
    other = other if isinstance(other, dict) else {"ctx": other}
    return pltpu.make_async_remote_copy(
        src_ref=src, dst_ref=dst, send_sem=send, recv_sem=recv,
        device_id=other, device_id_type=MESH,
    )


def gather_kernel(
    ring, rows_y, chosen_ref, k_ref, v_ref, x_ref, slots_ref, wants_ref, index_ref, meta_ref, xg_ref,
    up, down, stage, work, want, want_smem, xt, near, xin,
    up_send, up_recv, down_send, down_recv, w_send, w_recv, s_send, s_recv, local_sem, smem_sem,
    x_send, x_recv, in_sem,
):
    half = ring // 2
    x, z, c = place(ring)
    cls = x * 2 + c
    above, below = along(ring, 1), along(ring, -1)
    loads = [
        pltpu.make_async_copy(k_ref, near.at[0], in_sem.at[0]),
        pltpu.make_async_copy(v_ref, near.at[1], in_sem.at[1]),
        pltpu.make_async_copy(x_ref, xin, in_sem.at[2]),
    ]
    for load in loads:
        load.start()
    greet(neighbours(ring) + [column_mate(t) for t in range(1, rows_y)])

    def up_copy(s, part, src=None):
        src = up.at[s - 1, part] if src is None else src
        return push(src, up.at[s, part], up_send.at[s, part], up_recv.at[s, part], above)

    def down_copy(s, part, src=None):
        src = down.at[s - 1, part] if src is None else src
        return push(src, down.at[s, part], down_send.at[s, part], down_recv.at[s, part], below)

    for part, ref in ((0, k_ref), (1, v_ref)):
        up_copy(0, part, ref).start()
        down_copy(0, part, ref).start()

    shape = (4, 8, 128)
    spot = lax.broadcasted_iota(jnp.int32, shape, 0) * 128 + lax.broadcasted_iota(jnp.int32, shape, 2)
    wanted = jnp.full(shape, -1, jnp.int32)
    index = jnp.zeros(shape, jnp.int32)
    owners = []
    for i in range(2 * KV_HEADS * CHOSEN_BLOCKS):
        choice = chosen_ref[i]
        active = choice >= 0
        block = jnp.maximum(choice, 0)
        owner = block // 2
        marked = jnp.where(active, owner, -1)
        rank = jnp.int32(0)
        for other in owners:
            rank = rank + jnp.where(other == marked, 1, 0)
        owners.append(marked)
        line = (owner // (2 * ring)) * 2 + lax.rem(owner, 2)
        entry = lax.rem(owner // 2, ring) * CAP + rank
        hit = spot == jnp.where(active, line * 128 + entry, -1)
        wanted = jnp.where(hit, lax.rem(block, 2) * KV_HEADS + i // CHOSEN_BLOCKS % KV_HEADS, wanted)
        index = jnp.where(hit, i, index)
        meta_ref[i] = jnp.where(active, line * ring * CAP + entry, 0)
        meta_ref[64 + i] = jnp.where(active, 1, 0)
    want[...] = wanted
    index_ref[...] = index

    def want_copy(j):
        other, other_cls = member(ring, j)
        return push(want.at[other_cls], wants_ref.at[j], w_send.at[j - 1], w_recv.at[j - 1], other)

    for j in (1, 2, 3):
        want_copy(j).start()
    wants_ref[0] = want[cls]

    y = lax.axis_index("dp") // 2
    lines = 16 * ring
    half_width = lines * rows_y

    def x_copy(t):
        return push(
            xt.at[t], xg_ref.at[:, :, pl.ds(pl.multiple_of(y * TOKENS, TOKENS), TOKENS)],
            x_send.at[t], x_recv.at[t], column_mate(t),
        )

    def keep_copy():
        return pltpu.make_async_copy(
            xt.at[0], xg_ref.at[:, :, pl.ds(pl.multiple_of(y * TOKENS, TOKENS), TOKENS)], x_send.at[0]
        )

    def deal(t):
        to = lax.rem(y + t, rows_y)
        line = lax.broadcasted_iota(jnp.int32, (lines, half_width), 0)
        column = lax.broadcasted_iota(jnp.int32, (lines, half_width), 1)
        core, high, rest = line // (8 * ring), line // (4 * ring) % 2, line % (4 * ring)
        source = rest // 4 * (16 * rows_y) + core * (8 * rows_y) + to * 8 + high * 4 + rest % 4
        pick = jnp.where(column == source, 1.0, 0.0).astype(jnp.bfloat16)
        for lo in range(2):
            part = xin[:, lo * half_width : (lo + 1) * half_width]
            xt[t, lo] = lax.dot_general(
                pick, part, (((1,), (1,)), ((), ())), preferred_element_type=jnp.float32
            ).astype(jnp.bfloat16)

    for load in loads:
        load.wait()
    for j in (1, 2, 3):
        want_copy(j).wait()
    table = pltpu.make_async_copy(wants_ref, want_smem, smem_sem)
    table.start()
    table.wait()

    def slot_copy(j, r):
        owner = lax.rem(z + r, ring)
        return push(
            stage.at[r, j], slots_ref.at[cls, owner], s_send.at[j - 1, r], s_recv.at[j - 1, r],
            member(ring, j)[0],
        )

    def own_copy(r):
        return pltpu.make_async_copy(
            stage.at[r, 0], slots_ref.at[cls, lax.rem(z + r, ring)], local_sem.at[r]
        )

    def extract(r, keys, values):
        owner = lax.rem(z + r, ring)
        for b in range(2):
            for h in range(KV_HEADS):
                rows, lanes = pl.ds(b * BLOCK_LENGTH, BLOCK_LENGTH), pl.ds(h * HEAD_WIDTH, HEAD_WIDTH)
                work[b * KV_HEADS + h, :, :HEAD_WIDTH] = keys[rows, lanes]
                work[b * KV_HEADS + h, :, HEAD_WIDTH:] = values[rows, lanes]
        for j in (2, 3, 1, 0):
            for rank in range(CAP):
                unit = jnp.maximum(want_smem[j, 0, owner * CAP + rank], 0)
                stage[r, j, rank] = work[unit]
            if j:
                slot_copy(j, r).start()
        own_copy(r).start()

    extract(0, near.at[0], near.at[1])
    for t in range(rows_y):
        deal(t)
        if t == 0:
            keep_copy().start()
        else:
            x_copy(t).start()

    def step(s, _):
        for part in range(2):
            up_copy(s, part, k_ref).wait_recv()
            up_copy(s + 1, part).start()
            down_copy(s, part, k_ref).wait_recv()
            down_copy(s + 1, part).start()
        extract(ring - 1 - s, up.at[s, 0], up.at[s, 1])
        extract(1 + s, down.at[s, 0], down.at[s, 1])
        return 0

    lax.fori_loop(0, half - 2, step, 0)
    s = half - 2
    for part in range(2):
        up_copy(s, part, k_ref).wait_recv()
        if part == 0:
            up_copy(s + 1, part).start()
        down_copy(s, part, k_ref).wait_recv()
        if part == 1:
            down_copy(s + 1, part).start()
    extract(ring - 1 - s, up.at[s, 0], up.at[s, 1])
    extract(1 + s, down.at[s, 0], down.at[s, 1])
    up_copy(half - 1, 0, k_ref).wait_recv()
    down_copy(half - 1, 1, k_ref).wait_recv()
    extract(half, up.at[half - 1, 0], down.at[half - 1, 1])

    def drain(s, _):
        for part in range(2):
            up_copy(s, part, k_ref).wait_send()
            down_copy(s, part, k_ref).wait_send()
        return 0

    lax.fori_loop(0, half - 1, drain, 0)
    up_copy(half - 1, 0, k_ref).wait_send()
    down_copy(half - 1, 1, k_ref).wait_send()

    def drain_slots(r, _):
        for j in (1, 2, 3):
            slot_copy(j, r).wait()
        own_copy(r).wait()
        return 0

    lax.fori_loop(0, ring, drain_slots, 0)
    keep_copy().wait()
    for t in range(1, rows_y):
        x_copy(t).wait()


def gather_call(ring, rows_y, chosen, keys, values, inputs):
    half = ring // 2
    lines = 16 * ring
    ring_buffer = pltpu.VMEM((half, 2, TOKENS, KV_HEADS * HEAD_WIDTH), jnp.bfloat16)
    ring_sem = pltpu.SemaphoreType.DMA((half, 2))
    hbm, vmem = pl.BlockSpec(memory_space=pl.ANY), pl.BlockSpec(memory_space=pltpu.VMEM)
    smem = pl.BlockSpec(memory_space=pltpu.SMEM)
    dma = pltpu.SemaphoreType.DMA
    return pl.pallas_call(
        functools.partial(gather_kernel, ring, rows_y),
        out_shape=(
            jax.ShapeDtypeStruct((4, ring, CAP, BLOCK_LENGTH, PAIR), jnp.bfloat16),
            jax.ShapeDtypeStruct((4, 8, 128), jnp.int32),
            jax.ShapeDtypeStruct((4, 8, 128), jnp.int32),
            jax.ShapeDtypeStruct((128,), jnp.int32),
            jax.ShapeDtypeStruct((2, lines, rows_y * TOKENS), jnp.bfloat16),
        ),
        in_specs=[smem, hbm, hbm, hbm],
        out_specs=(hbm, vmem, vmem, smem, vmem),
        scratch_shapes=[
            ring_buffer,
            ring_buffer,
            pltpu.VMEM((ring, 4, CAP, BLOCK_LENGTH, PAIR), jnp.bfloat16),
            pltpu.VMEM((UNITS, BLOCK_LENGTH, PAIR), jnp.bfloat16),
            pltpu.VMEM((4, 8, 128), jnp.int32),
            pltpu.SMEM((4, 8, 128), jnp.int32),
            pltpu.VMEM((rows_y, 2, lines, TOKENS), jnp.bfloat16),
            pltpu.VMEM((2,) + keys.shape, jnp.bfloat16),
            pltpu.VMEM(inputs.shape, jnp.bfloat16),
            ring_sem, ring_sem, ring_sem, ring_sem,
            dma((3,)), dma((3,)), dma((3, ring)), dma((3, ring)), dma((ring,)), dma,
            dma((rows_y,)), dma((rows_y,)), dma((3,)),
        ],
        compiler_params=pltpu.CompilerParams(
            collective_id=0, has_side_effects=True, vmem_limit_bytes=VMEM_BYTES
        ),
        name="gather_blocks",
    )(chosen, keys, values, inputs)


def attend_kernel(
    meta_ref, q_ref, g_ref, k_ref, v_ref, lse_ref, delta_ref, slots_ref,
    dq_ref, dk_ref, dv_ref, part_ref, q, g, k, v, far, in_sem, far_sem,
):
    scale = HEAD_WIDTH ** (-0.5)
    inputs = [
        pltpu.make_async_copy(src, dst, in_sem.at[i])
        for i, (src, dst) in enumerate(((q_ref, q), (g_ref, g), (k_ref, k), (v_ref, v)))
    ]
    number = 2 * KV_HEADS * CHOSEN_BLOCKS
    fetches = [
        pltpu.make_async_copy(slots_ref.at[meta_ref[i]], far.at[i], far_sem.at[i])
        for i in range(number)
    ]
    for copy in inputs + fetches:
        copy.start()
    lse, delta = lse_ref[...].astype(jnp.float32), delta_ref[...].astype(jnp.float32)
    rows_n = GROUP * BLOCK_LENGTH
    nt = (((1,), (1,)), ((), ()))
    tn = (((0,), (0,)), ((), ()))

    def line(stat, h, b):
        return jnp.concatenate(
            [
                stat[h * GROUP + i : h * GROUP + i + 1, b * BLOCK_LENGTH : (b + 1) * BLOCK_LENGTH]
                for i in range(GROUP)
            ],
            axis=1,
        )

    def stack(ref, h, b):
        rows = slice(b * BLOCK_LENGTH, (b + 1) * BLOCK_LENGTH)
        heads = [h * GROUP + i for i in range(GROUP)]
        return jnp.concatenate(
            [ref[rows, i * HEAD_WIDTH : (i + 1) * HEAD_WIDTH] for i in heads], axis=0
        )

    for copy in inputs + fetches:
        copy.wait()
    for h in range(KV_HEADS):
        lanes = slice(h * HEAD_WIDTH, (h + 1) * HEAD_WIDTH)
        for b in range(2):
            first = (b * KV_HEADS + h) * CHOSEN_BLOCKS
            local = (b + 1) * BLOCK_LENGTH
            keys_n = local + CHOSEN_BLOCKS * BLOCK_LENGTH
            queries, grads = stack(q, h, b), stack(g, h, b)
            chosen = [far[first + i] for i in range(CHOSEN_BLOCKS)]
            keys = jnp.concatenate([k[:local, lanes]] + [f[:, :HEAD_WIDTH] for f in chosen], axis=0)
            values = jnp.concatenate([v[:local, lanes]] + [f[:, HEAD_WIDTH:] for f in chosen], axis=0)
            row = lax.broadcasted_iota(jnp.int32, (keys_n, rows_n), 1) % BLOCK_LENGTH
            key = lax.broadcasted_iota(jnp.int32, (keys_n, rows_n), 0)
            mask = (key < local) & (key <= row + b * BLOCK_LENGTH)
            for i in range(CHOSEN_BLOCKS):
                begin = local + i * BLOCK_LENGTH
                limit = jnp.where(meta_ref[64 + first + i] > 0, begin + BLOCK_LENGTH, begin)
                mask = mask | ((key >= begin) & (key < limit))
            scores = lax.dot_general(keys, queries, nt, preferred_element_type=jnp.float32) * scale
            prob = jnp.where(mask, jnp.exp(scores - line(lse, h, b)), 0.0)
            dprob = lax.dot_general(values, grads, nt, preferred_element_type=jnp.float32)
            dscore = (prob * (dprob - line(delta, h, b))).astype(jnp.bfloat16)
            prob_low = prob.astype(jnp.bfloat16)
            dq = lax.dot_general(dscore, keys, tn, preferred_element_type=jnp.float32) * scale
            dq = dq.astype(jnp.bfloat16)
            for i in range(GROUP):
                head = h * GROUP + i
                dq_ref[
                    b * BLOCK_LENGTH : (b + 1) * BLOCK_LENGTH,
                    head * HEAD_WIDTH : (head + 1) * HEAD_WIDTH,
                ] = dq[i * BLOCK_LENGTH : (i + 1) * BLOCK_LENGTH]
            dk = jnp.dot(dscore, queries, preferred_element_type=jnp.float32) * scale
            dv = jnp.dot(prob_low, grads, preferred_element_type=jnp.float32)
            for out, grad in ((dk_ref, dk), (dv_ref, dv)):
                if b == 0:
                    out[:BLOCK_LENGTH, lanes] = grad[:BLOCK_LENGTH]
                else:
                    out[:BLOCK_LENGTH, lanes] += grad[:BLOCK_LENGTH]
                    out[BLOCK_LENGTH:, lanes] = grad[BLOCK_LENGTH : 2 * BLOCK_LENGTH]
            for i in range(CHOSEN_BLOCKS):
                begin = local + i * BLOCK_LENGTH
                part_ref[0, first + i] = dk[begin : begin + BLOCK_LENGTH].astype(jnp.bfloat16)
                part_ref[1, first + i] = dv[begin : begin + BLOCK_LENGTH].astype(jnp.bfloat16)


def attend_call(meta, queries, grads, keys, values, lse, delta, slots):
    number = 2 * KV_HEADS * CHOSEN_BLOCKS
    hbm, vmem = pl.BlockSpec(memory_space=pl.ANY), pl.BlockSpec(memory_space=pltpu.VMEM)
    smem = pl.BlockSpec(memory_space=pltpu.SMEM)
    return pl.pallas_call(
        attend_kernel,
        in_specs=[smem, hbm, hbm, hbm, hbm, vmem, vmem, hbm],
        out_specs=(vmem,) * 4,
        out_shape=(
            jax.ShapeDtypeStruct(queries.shape, jnp.bfloat16),
            jax.ShapeDtypeStruct(keys.shape, jnp.float32),
            jax.ShapeDtypeStruct(keys.shape, jnp.float32),
            jax.ShapeDtypeStruct((2, number, BLOCK_LENGTH, HEAD_WIDTH), jnp.bfloat16),
        ),
        scratch_shapes=[
            pltpu.VMEM(queries.shape, jnp.bfloat16),
            pltpu.VMEM(queries.shape, jnp.bfloat16),
            pltpu.VMEM(keys.shape, jnp.bfloat16),
            pltpu.VMEM(keys.shape, jnp.bfloat16),
            pltpu.VMEM((number, BLOCK_LENGTH, PAIR), jnp.bfloat16),
            pltpu.SemaphoreType.DMA((4,)),
            pltpu.SemaphoreType.DMA((number,)),
        ],
        compiler_params=pltpu.CompilerParams(vmem_limit_bytes=VMEM_BYTES),
        name="attend_blocks",
    )(meta, queries, grads, keys, values, lse, delta, slots)


def reduce_kernel(
    ring, rows_y, weight_scale,
    part_ref, wants_ref, index_ref, dk_ref, dv_ref, xg_ref, kg_ref, vg_ref, wg_ref,
    up, down, ups, downs, arrived, stage, mine, want_smem, index_smem,
    all_k, own, across, shared, from_x, pieces, from_z,
    up_send, up_recv, down_send, down_recv, s_send, s_recv, smem_sem,
    y_send, y_recv, c_send, c_recv, x_send, x_recv, z_send, z_recv,
):
    half = ring // 2
    x, z, c = place(ring)
    high = lax.rem(lax.axis_index("dp"), 2)
    cls = x * 2 + c
    above, below = along(ring, 1), along(ring, -1)
    far_x = [row_mate(ring, j)[0] for j in (1, 3)]
    far_z = [{"ctx": along(ring, d)} for d in range(2, ring - 1)]
    tables = [
        pltpu.make_async_copy(wants_ref, want_smem, smem_sem.at[0]),
        pltpu.make_async_copy(index_ref, index_smem, smem_sem.at[1]),
    ]
    for table in tables:
        table.start()
    greet(neighbours(ring) + [column_mate(t) for t in range(1, rows_y)] + far_x + far_z)
    for table in tables:
        table.wait()

    def slot_copy(part, j, r):
        return push(
            stage.at[part, j - 1, r], arrived.at[part, j - 1, r],
            s_send.at[part, j - 1, r], s_recv.at[part, j - 1, r], member(ring, j)[0],
        )

    def term_of(part, line, owner, rank):
        return part_ref[part, index_smem[line, 0, owner * CAP + rank]]

    def send_slots(part, r):
        owner = lax.rem(z + r, ring)
        for j in (2, 3, 1):
            line = member(ring, j)[1]
            for rank in range(CAP):
                stage[part, j - 1, r, rank] = term_of(part, line, owner, rank)
            slot_copy(part, j, r).start()

    def both(act, part, s):
        act(part, half - s)
        pl.when((s > 0) & (s < half))(lambda: act(part, half + s))

    def up_copy(part, s, b):
        return push(
            ups.at[part, s, b], up.at[part, s, b], up_send.at[part, s, b], up_recv.at[part, s, b], above
        )

    def down_copy(part, s, b):
        return push(
            downs.at[part, s, b], down.at[part, s, b],
            down_send.at[part, s, b], down_recv.at[part, s, b], below,
        )

    def gather_terms(part, r):
        for j in (1, 2, 3):
            slot_copy(part, j, r).wait_recv()
        owner = lax.rem(z + r, ring)
        units = [[want_smem[j, 0, owner * CAP + rank] for rank in range(CAP)] for j in range(4)]
        for b in range(2):
            for h in range(KV_HEADS):
                acc = jnp.zeros((BLOCK_LENGTH, HEAD_WIDTH), jnp.float32)
                for j in range(4):
                    for rank in range(CAP):
                        if j == 0:
                            term = term_of(part, cls, owner, rank)
                        else:
                            term = arrived[part, j - 1, r, rank]
                        hit = units[j][rank] == b * KV_HEADS + h
                        acc = acc + jnp.where(hit, term.astype(jnp.float32), 0.0)
                mine[part, r, b, :, h * HEAD_WIDTH : (h + 1) * HEAD_WIDTH] = acc

    def first(part):
        ups[part, 0, 0] = mine[part, half, 0].astype(jnp.bfloat16)
        up_copy(part, 0, 0).start()
        downs[part, 0, 1] = mine[part, half, 1].astype(jnp.bfloat16)
        down_copy(part, 0, 1).start()

    def hop(part, s):
        up_copy(part, s - 1, 0).wait_recv()
        ups[part, s, 0] = (up[part, s - 1, 0].astype(jnp.float32) + mine[part, half - s, 0]).astype(
            jnp.bfloat16
        )
        up_copy(part, s, 0).start()
        down_copy(part, s - 1, 1).wait_recv()
        downs[part, s, 1] = (
            down[part, s - 1, 1].astype(jnp.float32) + mine[part, half + s, 1]
        ).astype(jnp.bfloat16)
        down_copy(part, s, 1).start()

        @pl.when(s > 1)
        def _():
            up_copy(part, s - 1, 1).wait_recv()

        ups[part, s, 1] = (up[part, s - 1, 1].astype(jnp.float32) + mine[part, half - s, 1]).astype(
            jnp.bfloat16
        )
        up_copy(part, s, 1).start()

        @pl.when(s > 1)
        def _():
            down_copy(part, s - 1, 0).wait_recv()

        downs[part, s, 0] = (
            down[part, s - 1, 0].astype(jnp.float32) + mine[part, half + s, 0]
        ).astype(jnp.bfloat16)
        down_copy(part, s, 0).start()

    def last(part):
        near, outs = ((dk_ref, (kg_ref, own)), (dv_ref, (vg_ref,)))[part]
        for b in range(2):
            up_copy(part, half - 1, b).wait_recv()
            down_copy(part, half - 1, b).wait_recv()
            rows = slice(b * BLOCK_LENGTH, (b + 1) * BLOCK_LENGTH)
            value = near[rows] + mine[part, 0, b]
            value = value + up[part, half - 1, b].astype(jnp.float32)
            value = value + down[part, half - 1, b].astype(jnp.float32)
            for out in outs:
                out[rows] = value.astype(jnp.bfloat16)

    for s in range(AHEAD + 1):
        both(send_slots, 0, s)
        if s >= LAG:
            both(send_slots, 1, s - LAG)
    blank = jnp.zeros((BLOCK_LENGTH, KV_HEADS * HEAD_WIDTH), jnp.bfloat16)
    for part in range(2):
        up[part, 0, 1] = blank
        down[part, 0, 0] = blank

    y = lax.axis_index("dp") // 2

    def y_copy(t):
        return push(own, all_k.at[y], y_send.at[t - 1], y_recv.at[t - 1], column_mate(t))

    def c_copy():
        return push(across.at[:, 1 - c], shared, c_send, c_recv, member(ring, 1)[0])

    def x_copy(j):
        mate, lo, hi = row_mate(ring, j)
        return push(
            across.at[lo, c, hi], from_x.at[j - 1], x_send.at[j - 1], x_recv.at[j - 1], mate
        )

    def z_copy(d):
        return push(
            pieces.at[lax.rem(z + d, ring)], from_z.at[d - 1],
            z_send.at[d - 1], z_recv.at[d - 1], along(ring, d),
        )

    def start_weights():
        for t in range(1, rows_y):
            y_copy(t).start()
        all_k[y] = own[...]

    def multiply():
        for t in range(1, rows_y):
            y_copy(t).wait_recv()
        gathered = all_k[...].reshape(rows_y * TOKENS, KV_HEADS * HEAD_WIDTH)
        for lo in range(2):
            product = jnp.dot(xg_ref[lo], gathered, preferred_element_type=jnp.float32)
            for core in range(2):
                for hi in range(2):
                    begin = (core * 2 + hi) * 4 * ring
                    across[lo, core, hi] = product[begin : begin + 4 * ring]
        c_copy().start()

    def add_core():
        c_copy().wait()
        for lo in range(2):
            for hi in range(2):
                across[lo, c, hi] += shared[lo, hi]
        for j in (1, 2, 3):
            x_copy(j).start()

    def add_row():
        for j in (1, 2, 3):
            x_copy(j).wait()
        value = across[x, c, high] + from_x[0] + from_x[1] + from_x[2]
        for i in range(ring):
            pieces[i] = value[4 * i : 4 * i + 4]
        for d in range(1, ring):
            z_copy(d).start()

    gather_terms(0, half)
    first(0)
    both(gather_terms, 0, 1)
    after = {half: start_weights, half + 2: multiply, half + 3: add_core}
    end = half + LAG
    after = {t: act for t, act in after.items() if t < end}

    def step(t, _):
        pl.when(t < half)(lambda: hop(0, t))
        pl.when(t == LAG)(lambda: first(1))
        pl.when(t > LAG)(lambda: hop(1, t - LAG))
        pl.when(t == half)(lambda: last(0))
        for at, act in after.items():
            pl.when(t == at)(act)
        pl.when(t + AHEAD <= half)(lambda: both(send_slots, 0, t + AHEAD))
        pl.when((t + AHEAD >= LAG) & (t + AHEAD <= end))(lambda: both(send_slots, 1, t + AHEAD - LAG))
        pl.when(t + 1 <= half)(lambda: both(gather_terms, 0, t + 1))
        pl.when((t + 1 >= LAG) & (t + 1 <= end))(lambda: both(gather_terms, 1, t + 1 - LAG))
        return 0

    lax.fori_loop(1, end, step, 0)
    for at, act in ((half, start_weights), (half + 2, multiply), (half + 3, add_core)):
        if at not in after:
            act()
    last(1)
    add_row()
    value = pieces[z]
    for d in range(1, ring):
        z_copy(d).wait_recv()
        value = value + from_z[d - 1]
    wg_ref[...] = value * weight_scale

    for t in range(1, rows_y):
        y_copy(t).wait_send()
    for d in range(1, ring):
        z_copy(d).wait_send()
    for part in range(2):
        up_copy(part, 0, 0).wait_send()
        down_copy(part, 0, 1).wait_send()

        def drain(s, _):
            for b in range(2):
                up_copy(part, s, b).wait_send()
                down_copy(part, s, b).wait_send()
            return 0

        lax.fori_loop(1, half, drain, 0)

        def drain_slots(r, _):
            for j in (1, 2, 3):
                slot_copy(part, j, r).wait_send()
            return 0

        lax.fori_loop(0, ring, drain_slots, 0)


def reduce_call(ring, rows_y, weight_scale, parts, wants, index, dk, dv, xg):
    half = ring // 2
    width = KV_HEADS * HEAD_WIDTH
    ring_buffer = pltpu.VMEM((2, half, 2, BLOCK_LENGTH, width), jnp.bfloat16)
    ring_sem = pltpu.SemaphoreType.DMA((2, half, 2))
    dma = pltpu.SemaphoreType.DMA
    return pl.pallas_call(
        functools.partial(reduce_kernel, ring, rows_y, weight_scale),
        out_shape=(
            jax.ShapeDtypeStruct((TOKENS, width), jnp.bfloat16),
            jax.ShapeDtypeStruct((TOKENS, width), jnp.bfloat16),
            jax.ShapeDtypeStruct((4, width), jnp.float32),
        ),
        in_specs=[pl.BlockSpec(memory_space=pltpu.VMEM)] * 6,
        out_specs=(pl.BlockSpec(memory_space=pltpu.VMEM),) * 3,
        scratch_shapes=[
            ring_buffer, ring_buffer, ring_buffer, ring_buffer,
            pltpu.VMEM((2, 3, ring, CAP, BLOCK_LENGTH, HEAD_WIDTH), jnp.bfloat16),
            pltpu.VMEM((2, 3, ring, CAP, BLOCK_LENGTH, HEAD_WIDTH), jnp.bfloat16),
            pltpu.VMEM((2, ring, 2, BLOCK_LENGTH, width), jnp.float32),
            pltpu.SMEM((4, 8, 128), jnp.int32),
            pltpu.SMEM((4, 8, 128), jnp.int32),
            pltpu.VMEM((rows_y, TOKENS, width), jnp.bfloat16),
            pltpu.VMEM((TOKENS, width), jnp.bfloat16),
            pltpu.VMEM((2, 2, 2, 4 * ring, width), jnp.float32),
            pltpu.VMEM((2, 2, 4 * ring, width), jnp.float32),
            pltpu.VMEM((3, 4 * ring, width), jnp.float32),
            pltpu.VMEM((ring, 4, width), jnp.float32),
            pltpu.VMEM((ring - 1, 4, width), jnp.float32),
            ring_sem, ring_sem, ring_sem, ring_sem,
            dma((2, 3, ring)), dma((2, 3, ring)), dma((2,)),
            dma((rows_y - 1,)), dma((rows_y - 1,)), dma, dma,
            dma((3,)), dma((3,)), dma((ring - 1,)), dma((ring - 1,)),
        ],
        compiler_params=pltpu.CompilerParams(
            collective_id=1, has_side_effects=True, vmem_limit_bytes=VMEM_BYTES
        ),
        name="reduce_blocks",
    )(parts, wants, index, dk, dv, xg)


def body(
    query_states,
    key_activations,
    value_activations,
    out_grad,
    logsumexp,
    row_delta,
    layer_input,
    chosen,
):
    shards = lax.axis_size("ctx")
    replicas = lax.axis_size("dp")
    ring = shards // 4
    rows_y = replicas // 2
    keys, values = key_activations[0], value_activations[0]
    slots, wants, index, meta, xg = gather_call(
        ring, rows_y, chosen[0].reshape(-1), keys, values, layer_input[0]
    )
    query_grad, dk, dv, parts = attend_call(
        meta, query_states[0], out_grad[0], keys, values, logsumexp[0], row_delta[0],
        slots.reshape(4 * ring * CAP, BLOCK_LENGTH, PAIR),
    )
    weight_scale = 1.0 / math.sqrt(TOKENS * shards * replicas)
    key_gradient, value_gradient, key_weight_grad = reduce_call(
        ring, rows_y, weight_scale, parts, wants, index, dk, dv, xg
    )
    return (query_grad[None], key_gradient[None], value_gradient[None], key_weight_grad)


def solution(mesh):
    seq = P("dp", "ctx", None)
    stat = P("dp", None, "ctx")
    return jax.shard_map(
        body,
        mesh=mesh,
        in_specs=(seq, seq, seq, seq, stat, stat, seq, P("dp", "ctx", None, None)),
        out_specs=(seq, seq, seq, P(("ctx", "dp"), None)),
        check_vma=False,
    )
```

time: 173 us -> 163 us (0.942)
  Pallas kernels: 161 us -> 155 us
  local copies, waits for them, and re-layouts: 9.53 us -> 5.81 us
    pallas_call x1, Pallas kernels: 90.9 us -> 82.5 us  [reduce_call(): pl.pallas_call(functools.partial(reduce_kernel, ring, rows_y, weight_scal...]
    pallas_call x1, Pallas kernels: 62.6 us -> 65.1 us  [gather_call(): pl.pallas_call(functools.partial(gather_kernel, ring, rows_y), out_shape=...]
    unnamed x14 -> x4, local copies, waits for them, and re-layouts: 7.61 us -> 5.21 us
    convert_element_type x6 -> x0, local copies, waits for them, and re-layouts: 1.73 us -> none  [blockwise(): return stat[0].reshape(KV_HEADS, GROUP, 2, BLOCK_LENGTH).transpose(2, 0,...]
where the time goes in v3:
time: 163 us; the launch traced here: 162 us
  Pallas kernels  155 us (95%)
  local copies, waits for them, and re-layouts  5.81 us (4%)
    pallas_call x1, Pallas kernels, reduce_call(): pl.pallas_call(functools.partial(reduce_kernel, ring, rows_y, weight_scal...  82.5 us
    pallas_call x1, Pallas kernels, gather_call(): pl.pallas_call(functools.partial(gather_kernel, ring, rows_y), out_shape=...  65.1 us
    pallas_call x1, Pallas kernels, attend_call(): pl.pallas_call(attend_kernel, in_specs=[smem, hbm, hbm, hbm, hbm, vmem, v...  7.9 us
    unnamed x4, local copies, waits for them, and re-layouts  5.21 us

profile of v3, /device:TPU:24, one launch (start us, length us, event | category | flops | bytes accessed | tf_op | source)
XLA Modules:
  0.0 161.9 jit_solution(9507792288629841445)
XLA Ops:
  0.6 0.8 copy.13
  1.4 0.6 reshape_squeeze.3.chosen_ref
  2.0 65.1 %gather_blocks.1 = (bf16[4,16,2,64,256]{4,3,2,1,0:T(8,128)(2,1)}, s32[4,8,128]{2,1,0:T(8,128)}, s32[4,8,128]{2,1,0:T(8,128)}, s32[128]{0:T(128)}, bf16[2,256,512]{2,1,0:T(8,128)(2,1)}) custom-call(s32[24]{0:T(128)} %reshape_squeeze.3.chosen_ref, bf16[128,512]{1,0:T(8,128)(2,1)} %bitcast.13, bf16[128,512]{1,0:T(8,128)(2,1)} %bitcast.15, ...), custom_call_target="tpu_custom_call" | custom-call | tf_op jit(solution)/shard_map/gather_blocks/pallas_call | solution.py:266
  67.1 7.9 %attend_blocks.1 = (bf16[128,2048]{1,0:T(8,128)(2,1)}, f32[128,512]{1,0:T(8,128)}, f32[128,512]{1,0:T(8,128)}, bf16[2,24,64,128]{3,2,1,0:T(8,128)(2,1)}) custom-call(s32[128]{0:T(128)} %get-tuple-element.16.meta_ref, bf16[128,2048]{1,0:T(8,128)(2,1)} %bitcast.17, bf16[128,2048]{1,0:T(8,128)(2,1)} %bitcast.18, bf16[128,512]{1,0:T(8,128)(2,1)} %bitcast.14, ...), custom_call_target="tpu_custom_call" | custom-call | tf_op jit(solution)/shard_map/attend_blocks/pallas_call | solution.py:385
  75.0 82.5 %reduce_blocks.1 = (bf16[128,512]{1,0:T(8,128)(2,1)}, bf16[128,512]{1,0:T(8,128)(2,1)}, f32[4,512]{1,0:T(4,128)}) custom-call(bf16[2,24,64,128]{3,2,1,0:T(8,128)(2,1)} %get-tuple-element.19.part_ref, s32[4,8,128]{2,1,0:T(8,128)} %get-tuple-element.20.wants_ref, s32[4,8,128]{2,1,0:T(8,128)} %get-tuple-element.21.index_ref, ...), custom_call_target="tpu_custom_call" | custom-call | tf_op jit(solution)/shard_map/reduce_blocks/pallas_call | solution.py:657
  157.5 1.6 copy.17
  159.0 1.6 copy.18
  160.6 1.3 copy.19

commit v4 on v3

--- a/solution.py
+++ b/solution.py
@@ -17,9 +17,11 @@
 TOKENS = 128
 UNITS = TOKENS // BLOCK_LENGTH * KV_HEADS
 PAIR = 2 * HEAD_WIDTH
-LAG = 4
+LAG = 5
 AHEAD = 3
+MULTIPLY, ADD_CORE, ADD_ROW = 2, 3, 4
 VMEM_BYTES = 58 * 1024 * 1024
+GATHER_INPUT, GATHER_SCRATCH = 6, 17
 MESH = pl.DeviceIdType.MESH
 
 
@@ -73,24 +75,16 @@
     )
 
 
-def gather_kernel(
-    ring, rows_y, chosen_ref, k_ref, v_ref, x_ref, slots_ref, wants_ref, index_ref, meta_ref, xg_ref,
-    up, down, stage, work, want, want_smem, xt, near, xin,
-    up_send, up_recv, down_send, down_recv, w_send, w_recv, s_send, s_recv, local_sem, smem_sem,
-    x_send, x_recv, in_sem,
+def gather_stage(
+    ring, rows_y, chosen_ref, k_ref, v_ref, x_ref, slots, wants, index, meta, want_smem, xg, near,
+    up, down, stage, work, want, xt, xin,
+    up_send, up_recv, down_send, down_recv, w_send, w_recv, s_send, s_recv, x_send, x_recv,
+    smem_sem, in_sem,
 ):
     half = ring // 2
     x, z, c = place(ring)
     cls = x * 2 + c
     above, below = along(ring, 1), along(ring, -1)
-    loads = [
-        pltpu.make_async_copy(k_ref, near.at[0], in_sem.at[0]),
-        pltpu.make_async_copy(v_ref, near.at[1], in_sem.at[1]),
-        pltpu.make_async_copy(x_ref, xin, in_sem.at[2]),
-    ]
-    for load in loads:
-        load.start()
-    greet(neighbours(ring) + [column_mate(t) for t in range(1, rows_y)])
 
     def up_copy(s, part, src=None):
         src = up.at[s - 1, part] if src is None else src
@@ -107,7 +101,7 @@
     shape = (4, 8, 128)
     spot = lax.broadcasted_iota(jnp.int32, shape, 0) * 128 + lax.broadcasted_iota(jnp.int32, shape, 2)
     wanted = jnp.full(shape, -1, jnp.int32)
-    index = jnp.zeros(shape, jnp.int32)
+    spots = jnp.zeros(shape, jnp.int32)
     owners = []
     for i in range(2 * KV_HEADS * CHOSEN_BLOCKS):
         choice = chosen_ref[i]
@@ -123,19 +117,19 @@
         entry = lax.rem(owner // 2, ring) * CAP + rank
         hit = spot == jnp.where(active, line * 128 + entry, -1)
         wanted = jnp.where(hit, lax.rem(block, 2) * KV_HEADS + i // CHOSEN_BLOCKS % KV_HEADS, wanted)
-        index = jnp.where(hit, i, index)
-        meta_ref[i] = jnp.where(active, line * ring * CAP + entry, 0)
-        meta_ref[64 + i] = jnp.where(active, 1, 0)
+        spots = jnp.where(hit, i, spots)
+        meta[i] = jnp.where(active, line * ring * CAP + entry, 0)
+        meta[64 + i] = jnp.where(active, 1, 0)
     want[...] = wanted
-    index_ref[...] = index
+    index[...] = spots
 
     def want_copy(j):
         other, other_cls = member(ring, j)
-        return push(want.at[other_cls], wants_ref.at[j], w_send.at[j - 1], w_recv.at[j - 1], other)
+        return push(want.at[other_cls], wants.at[j], w_send.at[j - 1], w_recv.at[j - 1], other)
 
     for j in (1, 2, 3):
         want_copy(j).start()
-    wants_ref[0] = want[cls]
+    wants[0] = want[cls]
 
     y = lax.axis_index("dp") // 2
     lines = 16 * ring
@@ -143,13 +137,13 @@
 
     def x_copy(t):
         return push(
-            xt.at[t], xg_ref.at[:, :, pl.ds(pl.multiple_of(y * TOKENS, TOKENS), TOKENS)],
+            xt.at[t], xg.at[:, :, pl.ds(pl.multiple_of(y * TOKENS, TOKENS), TOKENS)],
             x_send.at[t], x_recv.at[t], column_mate(t),
         )
 
     def keep_copy():
         return pltpu.make_async_copy(
-            xt.at[0], xg_ref.at[:, :, pl.ds(pl.multiple_of(y * TOKENS, TOKENS), TOKENS)], x_send.at[0]
+            xt.at[0], xg.at[:, :, pl.ds(pl.multiple_of(y * TOKENS, TOKENS), TOKENS)], x_send.at[0]
         )
 
     def deal(t):
@@ -165,24 +159,23 @@
                 pick, part, (((1,), (1,)), ((), ())), preferred_element_type=jnp.float32
             ).astype(jnp.bfloat16)
 
+    loads = [
+        pltpu.make_async_copy(src, dst, in_sem.at[i])
+        for i, (src, dst) in enumerate(((k_ref, near.at[0]), (v_ref, near.at[1]), (x_ref, xin)))
+    ]
     for load in loads:
         load.wait()
     for j in (1, 2, 3):
         want_copy(j).wait()
-    table = pltpu.make_async_copy(wants_ref, want_smem, smem_sem)
+    table = pltpu.make_async_copy(wants, want_smem, smem_sem.at[0])
     table.start()
     table.wait()
 
     def slot_copy(j, r):
         owner = lax.rem(z + r, ring)
         return push(
-            stage.at[r, j], slots_ref.at[cls, owner], s_send.at[j - 1, r], s_recv.at[j - 1, r],
-            member(ring, j)[0],
-        )
-
-    def own_copy(r):
-        return pltpu.make_async_copy(
-            stage.at[r, 0], slots_ref.at[cls, lax.rem(z + r, ring)], local_sem.at[r]
+            stage.at[r, j - 1], slots.at[pl.ds((cls * ring + owner) * CAP, CAP)],
+            s_send.at[j - 1, r], s_recv.at[j - 1, r], member(ring, j)[0],
         )
 
     def extract(r, keys, values):
@@ -195,10 +188,12 @@
         for j in (2, 3, 1, 0):
             for rank in range(CAP):
                 unit = jnp.maximum(want_smem[j, 0, owner * CAP + rank], 0)
-                stage[r, j, rank] = work[unit]
+                if j:
+                    stage[r, j - 1, rank] = work[unit]
+                else:
+                    slots[(cls * ring + owner) * CAP + rank] = work[unit]
             if j:
                 slot_copy(j, r).start()
-        own_copy(r).start()
 
     extract(0, near.at[0], near.at[1])
     for t in range(rows_y):
@@ -246,7 +241,6 @@
     def drain_slots(r, _):
         for j in (1, 2, 3):
             slot_copy(j, r).wait()
-        own_copy(r).wait()
         return 0
 
     lax.fori_loop(0, ring, drain_slots, 0)
@@ -255,62 +249,9 @@
         x_copy(t).wait()
 
 
-def gather_call(ring, rows_y, chosen, keys, values, inputs):
-    half = ring // 2
-    lines = 16 * ring
-    ring_buffer = pltpu.VMEM((half, 2, TOKENS, KV_HEADS * HEAD_WIDTH), jnp.bfloat16)
-    ring_sem = pltpu.SemaphoreType.DMA((half, 2))
-    hbm, vmem = pl.BlockSpec(memory_space=pl.ANY), pl.BlockSpec(memory_space=pltpu.VMEM)
-    smem = pl.BlockSpec(memory_space=pltpu.SMEM)
-    dma = pltpu.SemaphoreType.DMA
-    return pl.pallas_call(
-        functools.partial(gather_kernel, ring, rows_y),
-        out_shape=(
-            jax.ShapeDtypeStruct((4, ring, CAP, BLOCK_LENGTH, PAIR), jnp.bfloat16),
-            jax.ShapeDtypeStruct((4, 8, 128), jnp.int32),
-            jax.ShapeDtypeStruct((4, 8, 128), jnp.int32),
-            jax.ShapeDtypeStruct((128,), jnp.int32),
-            jax.ShapeDtypeStruct((2, lines, rows_y * TOKENS), jnp.bfloat16),
-        ),
-        in_specs=[smem, hbm, hbm, hbm],
-        out_specs=(hbm, vmem, vmem, smem, vmem),
-        scratch_shapes=[
-            ring_buffer,
-            ring_buffer,
-            pltpu.VMEM((ring, 4, CAP, BLOCK_LENGTH, PAIR), jnp.bfloat16),
-            pltpu.VMEM((UNITS, BLOCK_LENGTH, PAIR), jnp.bfloat16),
-            pltpu.VMEM((4, 8, 128), jnp.int32),
-            pltpu.SMEM((4, 8, 128), jnp.int32),
-            pltpu.VMEM((rows_y, 2, lines, TOKENS), jnp.bfloat16),
-            pltpu.VMEM((2,) + keys.shape, jnp.bfloat16),
-            pltpu.VMEM(inputs.shape, jnp.bfloat16),
-            ring_sem, ring_sem, ring_sem, ring_sem,
-            dma((3,)), dma((3,)), dma((3, ring)), dma((3, ring)), dma((ring,)), dma,
-            dma((rows_y,)), dma((rows_y,)), dma((3,)),
-        ],
-        compiler_params=pltpu.CompilerParams(
-            collective_id=0, has_side_effects=True, vmem_limit_bytes=VMEM_BYTES
-        ),
-        name="gather_blocks",
-    )(chosen, keys, values, inputs)
-
-
-def attend_kernel(
-    meta_ref, q_ref, g_ref, k_ref, v_ref, lse_ref, delta_ref, slots_ref,
-    dq_ref, dk_ref, dv_ref, part_ref, q, g, k, v, far, in_sem, far_sem,
-):
+def attend_stage(meta, lse_ref, delta_ref, slots, dq_ref, dk_ref, dv_ref, part_ref, q, g, near):
     scale = HEAD_WIDTH ** (-0.5)
-    inputs = [
-        pltpu.make_async_copy(src, dst, in_sem.at[i])
-        for i, (src, dst) in enumerate(((q_ref, q), (g_ref, g), (k_ref, k), (v_ref, v)))
-    ]
-    number = 2 * KV_HEADS * CHOSEN_BLOCKS
-    fetches = [
-        pltpu.make_async_copy(slots_ref.at[meta_ref[i]], far.at[i], far_sem.at[i])
-        for i in range(number)
-    ]
-    for copy in inputs + fetches:
-        copy.start()
+    k, v = near.at[0], near.at[1]
     lse, delta = lse_ref[...].astype(jnp.float32), delta_ref[...].astype(jnp.float32)
     rows_n = GROUP * BLOCK_LENGTH
     nt = (((1,), (1,)), ((), ()))
@@ -332,8 +273,6 @@
             [ref[rows, i * HEAD_WIDTH : (i + 1) * HEAD_WIDTH] for i in heads], axis=0
         )
 
-    for copy in inputs + fetches:
-        copy.wait()
     for h in range(KV_HEADS):
         lanes = slice(h * HEAD_WIDTH, (h + 1) * HEAD_WIDTH)
         for b in range(2):
@@ -341,7 +280,7 @@
             local = (b + 1) * BLOCK_LENGTH
             keys_n = local + CHOSEN_BLOCKS * BLOCK_LENGTH
             queries, grads = stack(q, h, b), stack(g, h, b)
-            chosen = [far[first + i] for i in range(CHOSEN_BLOCKS)]
+            chosen = [slots[meta[first + i]] for i in range(CHOSEN_BLOCKS)]
             keys = jnp.concatenate([k[:local, lanes]] + [f[:, :HEAD_WIDTH] for f in chosen], axis=0)
             values = jnp.concatenate([v[:local, lanes]] + [f[:, HEAD_WIDTH:] for f in chosen], axis=0)
             row = lax.broadcasted_iota(jnp.int32, (keys_n, rows_n), 1) % BLOCK_LENGTH
@@ -349,7 +288,7 @@
             mask = (key < local) & (key <= row + b * BLOCK_LENGTH)
             for i in range(CHOSEN_BLOCKS):
                 begin = local + i * BLOCK_LENGTH
-                limit = jnp.where(meta_ref[64 + first + i] > 0, begin + BLOCK_LENGTH, begin)
+                limit = jnp.where(meta[64 + first + i] > 0, begin + BLOCK_LENGTH, begin)
                 mask = mask | ((key >= begin) & (key < limit))
             scores = lax.dot_general(keys, queries, nt, preferred_element_type=jnp.float32) * scale
             prob = jnp.where(mask, jnp.exp(scores - line(lse, h, b)), 0.0)
@@ -378,40 +317,12 @@
                 part_ref[1, first + i] = dv[begin : begin + BLOCK_LENGTH].astype(jnp.bfloat16)
 
 
-def attend_call(meta, queries, grads, keys, values, lse, delta, slots):
-    number = 2 * KV_HEADS * CHOSEN_BLOCKS
-    hbm, vmem = pl.BlockSpec(memory_space=pl.ANY), pl.BlockSpec(memory_space=pltpu.VMEM)
-    smem = pl.BlockSpec(memory_space=pltpu.SMEM)
-    return pl.pallas_call(
-        attend_kernel,
-        in_specs=[smem, hbm, hbm, hbm, hbm, vmem, vmem, hbm],
-        out_specs=(vmem,) * 4,
-        out_shape=(
-            jax.ShapeDtypeStruct(queries.shape, jnp.bfloat16),
-            jax.ShapeDtypeStruct(keys.shape, jnp.float32),
-            jax.ShapeDtypeStruct(keys.shape, jnp.float32),
-            jax.ShapeDtypeStruct((2, number, BLOCK_LENGTH, HEAD_WIDTH), jnp.bfloat16),
-        ),
-        scratch_shapes=[
-            pltpu.VMEM(queries.shape, jnp.bfloat16),
-            pltpu.VMEM(queries.shape, jnp.bfloat16),
-            pltpu.VMEM(keys.shape, jnp.bfloat16),
-            pltpu.VMEM(keys.shape, jnp.bfloat16),
-            pltpu.VMEM((number, BLOCK_LENGTH, PAIR), jnp.bfloat16),
-            pltpu.SemaphoreType.DMA((4,)),
-            pltpu.SemaphoreType.DMA((number,)),
-        ],
-        compiler_params=pltpu.CompilerParams(vmem_limit_bytes=VMEM_BYTES),
-        name="attend_blocks",
-    )(meta, queries, grads, keys, values, lse, delta, slots)
-
-
-def reduce_kernel(
-    ring, rows_y, weight_scale,
-    part_ref, wants_ref, index_ref, dk_ref, dv_ref, xg_ref, kg_ref, vg_ref, wg_ref,
-    up, down, ups, downs, arrived, stage, mine, want_smem, index_smem,
+def reduce_stage(
+    ring, rows_y, weight_scale, part_ref, want_smem, index_smem, dk_ref, dv_ref, xg_ref,
+    kg_ref, vg_ref, wg_ref,
+    up, down, ups, downs, arrived, stage, mine,
     all_k, own, across, shared, from_x, pieces, from_z,
-    up_send, up_recv, down_send, down_recv, s_send, s_recv, smem_sem,
+    up_send, up_recv, down_send, down_recv, s_send, s_recv,
     y_send, y_recv, c_send, c_recv, x_send, x_recv, z_send, z_recv,
 ):
     half = ring // 2
@@ -419,17 +330,6 @@
     high = lax.rem(lax.axis_index("dp"), 2)
     cls = x * 2 + c
     above, below = along(ring, 1), along(ring, -1)
-    far_x = [row_mate(ring, j)[0] for j in (1, 3)]
-    far_z = [{"ctx": along(ring, d)} for d in range(2, ring - 1)]
-    tables = [
-        pltpu.make_async_copy(wants_ref, want_smem, smem_sem.at[0]),
-        pltpu.make_async_copy(index_ref, index_smem, smem_sem.at[1]),
-    ]
-    for table in tables:
-        table.start()
-    greet(neighbours(ring) + [column_mate(t) for t in range(1, rows_y)] + far_x + far_z)
-    for table in tables:
-        table.wait()
 
     def slot_copy(part, j, r):
         return push(
@@ -595,16 +495,18 @@
     gather_terms(0, half)
     first(0)
     both(gather_terms, 0, 1)
-    after = {half: start_weights, half + 2: multiply, half + 3: add_core}
+    jobs = (
+        (half, start_weights), (half + MULTIPLY, multiply), (half + ADD_CORE, add_core),
+        (half + ADD_ROW, add_row),
+    )
     end = half + LAG
-    after = {t: act for t, act in after.items() if t < end}
 
     def step(t, _):
         pl.when(t < half)(lambda: hop(0, t))
         pl.when(t == LAG)(lambda: first(1))
         pl.when(t > LAG)(lambda: hop(1, t - LAG))
         pl.when(t == half)(lambda: last(0))
-        for at, act in after.items():
+        for at, act in jobs:
             pl.when(t == at)(act)
         pl.when(t + AHEAD <= half)(lambda: both(send_slots, 0, t + AHEAD))
         pl.when((t + AHEAD >= LAG) & (t + AHEAD <= end))(lambda: both(send_slots, 1, t + AHEAD - LAG))
@@ -613,11 +515,10 @@
         return 0
 
     lax.fori_loop(1, end, step, 0)
-    for at, act in ((half, start_weights), (half + 2, multiply), (half + 3, add_core)):
-        if at not in after:
+    last(1)
+    for at, act in jobs:
+        if at >= end:
             act()
-    last(1)
-    add_row()
     value = pieces[z]
     for d in range(1, ring):
         z_copy(d).wait_recv()
@@ -648,45 +549,131 @@
         lax.fori_loop(0, ring, drain_slots, 0)
 
 
-def reduce_call(ring, rows_y, weight_scale, parts, wants, index, dk, dv, xg):
+def fused_kernel(
+    ring, rows_y, weight_scale, chosen_ref, k_ref, v_ref, x_ref, q_ref, g_ref, lse_ref, delta_ref,
+    dq_ref, kg_ref, vg_ref, wg_ref,
+    slots, wants, index, meta, want_smem, index_smem, xg, near, q, g, dk, dv, parts,
+    in_sem, smem_sem, *scratch,
+):
+    loads = [
+        pltpu.make_async_copy(src, dst, in_sem.at[i])
+        for i, (src, dst) in enumerate(
+            (
+                (k_ref, near.at[0]), (v_ref, near.at[1]), (x_ref, scratch[GATHER_INPUT]),
+                (q_ref, q), (g_ref, g),
+            )
+        )
+    ]
+    for load in loads:
+        load.start()
+    far_x = [row_mate(ring, j)[0] for j in (1, 3)]
+    far_z = [{"ctx": along(ring, d)} for d in range(2, ring - 1)]
+    greet(neighbours(ring) + [column_mate(t) for t in range(1, rows_y)] + far_x + far_z)
+    gather_stage(
+        ring, rows_y, chosen_ref, k_ref, v_ref, x_ref, slots, wants, index, meta, want_smem, xg, near,
+        *scratch[:GATHER_SCRATCH], smem_sem, in_sem,
+    )
+    table = pltpu.make_async_copy(index, index_smem, smem_sem.at[1])
+    table.start()
+    for load in loads[3:]:
+        load.wait()
+    attend_stage(meta, lse_ref, delta_ref, slots, dq_ref, dk, dv, parts, q, g, near)
+    table.wait()
+    reduce_stage(
+        ring, rows_y, weight_scale, parts, want_smem, index_smem, dk, dv, xg,
+        kg_ref, vg_ref, wg_ref, *scratch[GATHER_SCRATCH:],
+    )
+
+
+def fused_call(ring, rows_y, weight_scale, chosen, keys, values, inputs, queries, grads, lse, delta):
     half = ring // 2
+    lines = 16 * ring
     width = KV_HEADS * HEAD_WIDTH
-    ring_buffer = pltpu.VMEM((2, half, 2, BLOCK_LENGTH, width), jnp.bfloat16)
-    ring_sem = pltpu.SemaphoreType.DMA((2, half, 2))
+    number = 2 * KV_HEADS * CHOSEN_BLOCKS
+    hbm, vmem = pl.BlockSpec(memory_space=pl.ANY), pl.BlockSpec(memory_space=pltpu.VMEM)
+    smem = pl.BlockSpec(memory_space=pltpu.SMEM)
     dma = pltpu.SemaphoreType.DMA
+    low, full = jnp.bfloat16, jnp.float32
+    table = (4, 8, 128)
+    shared = [
+        pltpu.VMEM((4 * ring * CAP, BLOCK_LENGTH, PAIR), low),
+        pltpu.VMEM(table, jnp.int32),
+        pltpu.VMEM(table, jnp.int32),
+        pltpu.SMEM((128,), jnp.int32),
+        pltpu.SMEM(table, jnp.int32),
+        pltpu.SMEM(table, jnp.int32),
+        pltpu.VMEM((2, lines, rows_y * TOKENS), low),
+        pltpu.VMEM((2,) + keys.shape, low),
+        pltpu.VMEM(queries.shape, low),
+        pltpu.VMEM(queries.shape, low),
+        pltpu.VMEM(keys.shape, full),
+        pltpu.VMEM(keys.shape, full),
+        pltpu.VMEM((2, number, BLOCK_LENGTH, HEAD_WIDTH), low),
+        dma((5,)), dma((2,)),
+    ]
+    gather_ring, gather_sem = pltpu.VMEM((half, 2, TOKENS, width), low), dma((half, 2))
+    gather = [
+        gather_ring, gather_ring,
+        pltpu.VMEM((ring, 3, CAP, BLOCK_LENGTH, PAIR), low),
+        pltpu.VMEM((UNITS, BLOCK_LENGTH, PAIR), low),
+        pltpu.VMEM(table, jnp.int32),
+        pltpu.VMEM((rows_y, 2, lines, TOKENS), low),
+        pltpu.VMEM(inputs.shape, low),
+        gather_sem, gather_sem, gather_sem, gather_sem,
+        dma((3,)), dma((3,)), dma((3, ring)), dma((3, ring)), dma((rows_y,)), dma((rows_y,)),
+    ]
+    reduce_ring, reduce_sem = pltpu.VMEM((2, half, 2, BLOCK_LENGTH, width), low), dma((2, half, 2))
+    reduce = [
+        reduce_ring, reduce_ring, reduce_ring, reduce_ring,
+        pltpu.VMEM((2, 3, ring, CAP, BLOCK_LENGTH, HEAD_WIDTH), low),
+        pltpu.VMEM((2, 3, ring, CAP, BLOCK_LENGTH, HEAD_WIDTH), low),
+        pltpu.VMEM((2, ring, 2, BLOCK_LENGTH, width), full),
+        pltpu.VMEM((rows_y, TOKENS, width), low),
+        pltpu.VMEM((TOKENS, width), low),
+        pltpu.VMEM((2, 2, 2, 4 * ring, width), full),
+        pltpu.VMEM((2, 2, 4 * ring, width), full),
+        pltpu.VMEM((3, 4 * ring, width), full),
+        pltpu.VMEM((ring, 4, width), full),
+        pltpu.VMEM((ring - 1, 4, width), full),
+        reduce_sem, reduce_sem, reduce_sem, reduce_sem,
+        dma((2, 3, ring)), dma((2, 3, ring)),
+        dma((rows_y - 1,)), dma((rows_y - 1,)), dma, dma,
+        dma((3,)), dma((3,)), dma((ring - 1,)), dma((ring - 1,)),
+    ]
+    assert len(gather) == GATHER_SCRATCH
     return pl.pallas_call(
-        functools.partial(reduce_kernel, ring, rows_y, weight_scale),
+        functools.partial(fused_kernel, ring, rows_y, weight_scale),
         out_shape=(
-            jax.ShapeDtypeStruct((TOKENS, width), jnp.bfloat16),
-            jax.ShapeDtypeStruct((TOKENS, width), jnp.bfloat16),
-            jax.ShapeDtypeStruct((4, width), jnp.float32),
+            jax.ShapeDtypeStruct(queries.shape, low),
+            jax.ShapeDtypeStruct((TOKENS, width), low),
+            jax.ShapeDtypeStruct((TOKENS, width), low),
+            jax.ShapeDtypeStruct((4, width), full),
         ),
-        in_specs=[pl.BlockSpec(memory_space=pltpu.VMEM)] * 6,
-        out_specs=(pl.BlockSpec(memory_space=pltpu.VMEM),) * 3,
-        scratch_shapes=[
-            ring_buffer, ring_buffer, ring_buffer, ring_buffer,
-            pltpu.VMEM((2, 3, ring, CAP, BLOCK_LENGTH, HEAD_WIDTH), jnp.bfloat16),
-            pltpu.VMEM((2, 3, ring, CAP, BLOCK_LENGTH, HEAD_WIDTH), jnp.bfloat16),
-            pltpu.VMEM((2, ring, 2, BLOCK_LENGTH, width), jnp.float32),
-            pltpu.SMEM((4, 8, 128), jnp.int32),
-            pltpu.SMEM((4, 8, 128), jnp.int32),
-            pltpu.VMEM((rows_y, TOKENS, width), jnp.bfloat16),
-            pltpu.VMEM((TOKENS, width), jnp.bfloat16),
-            pltpu.VMEM((2, 2, 2, 4 * ring, width), jnp.float32),
-            pltpu.VMEM((2, 2, 4 * ring, width), jnp.float32),
-            pltpu.VMEM((3, 4 * ring, width), jnp.float32),
-            pltpu.VMEM((ring, 4, width), jnp.float32),
-            pltpu.VMEM((ring - 1, 4, width), jnp.float32),
-            ring_sem, ring_sem, ring_sem, ring_sem,
-            dma((2, 3, ring)), dma((2, 3, ring)), dma((2,)),
-            dma((rows_y - 1,)), dma((rows_y - 1,)), dma, dma,
-            dma((3,)), dma((3,)), dma((ring - 1,)), dma((ring - 1,)),
-        ],
+        in_specs=[smem, hbm, hbm, hbm, hbm, hbm, vmem, vmem],
+        out_specs=(vmem,) * 4,
+        scratch_shapes=shared + gather + reduce,
         compiler_params=pltpu.CompilerParams(
-            collective_id=1, has_side_effects=True, vmem_limit_bytes=VMEM_BYTES
+            collective_id=0, has_side_effects=True, vmem_limit_bytes=VMEM_BYTES
         ),
-        name="reduce_blocks",
-    )(parts, wants, index, dk, dv, xg)
+        name="fused_blocks",
+    )(chosen, keys, values, inputs, queries, grads, lse, delta)
+
+
+def hand_over_kernel(*refs):
+    n = len(refs) // 2
+    for i in range(n):
+        refs[n + i][...] = refs[i][...]
+
+
+def hand_over(*arrays):
+    vmem = pl.BlockSpec(memory_space=pltpu.VMEM)
+    return pl.pallas_call(
+        hand_over_kernel,
+        in_specs=[vmem] * len(arrays),
+        out_specs=(vmem,) * len(arrays),
+        out_shape=tuple(jax.ShapeDtypeStruct(a.shape, a.dtype) for a in arrays),
+        name="hand_over",
+    )(*arrays)
 
 
 def body(
@@ -704,17 +691,12 @@
     ring = shards // 4
     rows_y = replicas // 2
     keys, values = key_activations[0], value_activations[0]
-    slots, wants, index, meta, xg = gather_call(
-        ring, rows_y, chosen[0].reshape(-1), keys, values, layer_input[0]
+    weight_scale = 1.0 / math.sqrt(TOKENS * shards * replicas)
+    outputs = fused_call(
+        ring, rows_y, weight_scale, chosen[0].reshape(-1), keys, values, layer_input[0],
+        query_states[0], out_grad[0], logsumexp[0], row_delta[0],
     )
-    query_grad, dk, dv, parts = attend_call(
-        meta, query_states[0], out_grad[0], keys, values, logsumexp[0], row_delta[0],
-        slots.reshape(4 * ring * CAP, BLOCK_LENGTH, PAIR),
-    )
-    weight_scale = 1.0 / math.sqrt(TOKENS * shards * replicas)
-    key_gradient, value_gradient, key_weight_grad = reduce_call(
-        ring, rows_y, weight_scale, parts, wants, index, dk, dv, xg
-    )
+    query_grad, key_gradient, value_gradient, key_weight_grad = hand_over(*outputs)
     return (query_grad[None], key_gradient[None], value_gradient[None], key_weight_grad)
 
 

time: 163 us -> 150 us (0.920)
  Pallas kernels: 155 us -> 148 us
  local copies, waits for them, and re-layouts: 5.81 us -> 1.37 us
    pallas_call x3 -> x2, Pallas kernels: 155 us -> 148 us  [the longest x1 146 us: fused_call(): pl.pallas_call(functools.partial(fused_kernel, ring, rows_y, weight_scale...]
    unnamed x4 -> x3, local copies, waits for them, and re-layouts: 5.21 us -> 0.78 us
where the time goes in v4:
time: 150 us
  Pallas kernels  148 us (99%)
    pallas_call x1, Pallas kernels, fused_call(): pl.pallas_call(functools.partial(fused_kernel, ring, rows_y, weight_scale...  146 us

profile of v4, /device:TPU:24, one launch (start us, length us, event | category | flops | bytes accessed | tf_op | source)
XLA Modules:
  0.0 149.7 jit_solution(12864607091248816938)
XLA Ops:
  0.6 0.0 copy-start
  0.6 0.7 copy-done
  1.3 0.1 copy.13
  1.4 0.6 reshape_squeeze.3.chosen_ref
  2.0 145.7 %fused_blocks.1 = (bf16[128,2048]{1,0:T(8,128)(2,1)}, bf16[128,512]{1,0:T(8,128)(2,1)}, bf16[128,512]{1,0:T(8,128)(2,1)}, f32[4,512]{1,0:T(4,128)}) custom-call(s32[24]{0:T(128)} %reshape_squeeze.3.chosen_ref, bf16[128,512]{1,0:T(8,128)(2,1)} %bitcast.13, bf16[128,512]{1,0:T(8,128)(2,1)} %bitcast.14, bf16[128,2048]{1,0:T(8,128)(2,1)} %bitcast.10, ...), custom_call_target="tpu_custom_call" | custom-call | tf_op jit(solution)/shard_map/fused_blocks/pallas_call | solution.py:644
  147.7 2.0 %hand_over.1 = (bf16[128,2048]{1,0:T(8,128)(2,1)}, bf16[128,512]{1,0:T(8,128)(2,1)}, bf16[128,512]{1,0:T(8,128)(2,1)}, f32[4,512]{1,0:T(4,128)}) custom-call(bf16[128,2048]{1,0:T(8,128)(2,1)} %get-tuple-element.12.refs_0_, bf16[128,512]{1,0:T(8,128)(2,1)} %get-tuple-element.13.refs_1_, bf16[128,512]{1,0:T(8,128)(2,1)} %get-tuple-element.14.refs_2_, ...), custom_call_target="tpu_custom_call" | custom-call | tf_op jit(solution)/shard_map/hand_over/pallas_call | solution.py:670
Async XLA Ops:
  0.6 0.7 copy-start

commit v5 on v4

v5 whole, which is shorter than its diff:
```python
import functools
import math

import jax
import jax.numpy as jnp
from jax import lax
from jax.experimental import pallas as pl
from jax.experimental.pallas import tpu as pltpu
from jax.sharding import PartitionSpec as P

HEAD_WIDTH = 128
BLOCK_LENGTH = 64
CHOSEN_BLOCKS = 3
CAP = 2
KV_HEADS = 4
GROUP = 4
TOKENS = 128
UNITS = TOKENS // BLOCK_LENGTH * KV_HEADS
LAG = 5
AHEAD = 4
AHEAD_V = 4
MULTIPLY, ADD_CORE, ADD_ROW = 2, 3, 4
VMEM_BYTES = 58 * 1024 * 1024
GATHER_INPUT, GATHER_SCRATCH = 6, 17
MESH = pl.DeviceIdType.MESH


def place(ring):
    i = lax.axis_index("ctx")
    return i // (2 * ring), lax.rem(i // 2, ring), lax.rem(i, 2)


def member(ring, j):
    x, z, c = place(ring)
    mx = lax.rem(x + j // 2, 2)
    mc = lax.rem(c + j % 2, 2)
    return mx * (2 * ring) + z * 2 + mc, mx * 2 + mc


def along(ring, step):
    x, z, c = place(ring)
    return x * (2 * ring) + lax.rem(z + step + ring, ring) * 2 + c


def column_mate(step):
    i, d = lax.axis_index("ctx"), lax.axis_index("dp")
    rows = lax.axis_size("dp") // 2
    return {"ctx": i, "dp": lax.rem(d // 2 + step, rows) * 2 + lax.rem(d, 2)}


def row_mate(ring, j):
    x, z, c = place(ring)
    d = lax.axis_index("dp")
    lo, hi = lax.rem(x + j // 2, 2), lax.rem(lax.rem(d, 2) + j % 2, 2)
    return {"ctx": lo * (2 * ring) + z * 2 + c, "dp": d // 2 * 2 + hi}, lo, hi


def greet(others):
    barrier = pltpu.get_barrier_semaphore()
    for other in others:
        pl.semaphore_signal(barrier, inc=1, device_id=other, device_id_type=MESH)
    pl.semaphore_wait(barrier, len(others))


def neighbours(ring):
    places = [along(ring, 1), along(ring, -1)] + [member(ring, j)[0] for j in (1, 2, 3)]
    return [{"ctx": other} for other in places]


def push(src, dst, send, recv, other):
    other = other if isinstance(other, dict) else {"ctx": other}
    return pltpu.make_async_remote_copy(
        src_ref=src, dst_ref=dst, send_sem=send, recv_sem=recv,
        device_id=other, device_id_type=MESH,
    )


def gather_stage(
    ring, rows_y, chosen_ref, k_ref, v_ref, x_ref, q_ref, g_ref, q, g, slots, wants, index, meta, want_smem, xg, near,
    up, down, stage, work, want, xt, xin,
    up_send, up_recv, down_send, down_recv, w_send, w_recv, s_send, s_recv, x_send, x_recv,
    smem_sem, in_sem, local_part,
):
    half = ring // 2
    x, z, c = place(ring)
    cls = x * 2 + c
    above, below = along(ring, 1), along(ring, -1)

    def up_copy(s, part, b, src=None):
        at = (s, part, b)
        src = up.at[s - 1, part, b] if src is None else src
        return push(src, up.at[at], up_send.at[at], up_recv.at[at], above)

    def down_copy(s, part, b, src=None):
        at = (s, part, b)
        src = down.at[s - 1, part, b] if src is None else src
        return push(src, down.at[at], down_send.at[at], down_recv.at[at], below)

    some = k_ref.at[:BLOCK_LENGTH]
    for part, ref in ((0, k_ref), (1, v_ref)):
        for b in range(2):
            rows = ref.at[b * BLOCK_LENGTH : (b + 1) * BLOCK_LENGTH]
            up_copy(0, part, b, rows).start()
            down_copy(0, part, b, rows).start()

    shape = (4, 8, 128)
    spot = lax.broadcasted_iota(jnp.int32, shape, 0) * 128 + lax.broadcasted_iota(jnp.int32, shape, 2)
    wanted = jnp.full(shape, -1, jnp.int32)
    spots = jnp.zeros(shape, jnp.int32)
    owners = []
    for i in range(2 * KV_HEADS * CHOSEN_BLOCKS):
        choice = chosen_ref[i // (KV_HEADS * CHOSEN_BLOCKS), i // CHOSEN_BLOCKS % KV_HEADS, i % CHOSEN_BLOCKS]
        active = choice >= 0
        block = jnp.maximum(choice, 0)
        owner = block // 2
        marked = jnp.where(active, owner, -1)
        rank = jnp.int32(0)
        for other in owners:
            rank = rank + jnp.where(other == marked, 1, 0)
        owners.append(marked)
        line = (owner // (2 * ring)) * 2 + lax.rem(owner, 2)
        entry = lax.rem(owner // 2, ring) * CAP + rank
        hit = spot == jnp.where(active, line * 128 + entry, -1)
        wanted = jnp.where(hit, lax.rem(block, 2) * KV_HEADS + i // CHOSEN_BLOCKS % KV_HEADS, wanted)
        spots = jnp.where(hit, i, spots)
        meta[i] = jnp.where(active, line * ring * CAP + entry, 0)
        meta[64 + i] = jnp.where(active, 1, 0)
    want[...] = wanted
    index[...] = spots

    def want_copy(j):
        other, other_cls = member(ring, j)
        return push(want.at[other_cls], wants.at[j], w_send.at[j - 1], w_recv.at[j - 1], other)

    for j in (1, 2, 3):
        want_copy(j).start()
    wants[0] = want[cls]

    y = lax.axis_index("dp") // 2
    lines = 16 * ring
    half_width = lines * rows_y

    def x_copy(t):
        return push(
            xt.at[t], xg.at[:, :, pl.ds(pl.multiple_of(y * TOKENS, TOKENS), TOKENS)],
            x_send.at[t], x_recv.at[t], column_mate(t),
        )

    def keep_copy():
        return pltpu.make_async_copy(
            xt.at[0], xg.at[:, :, pl.ds(pl.multiple_of(y * TOKENS, TOKENS), TOKENS)], x_send.at[0]
        )

    def deal(t):
        to = lax.rem(y + t, rows_y)
        line = lax.broadcasted_iota(jnp.int32, (lines, half_width), 0)
        column = lax.broadcasted_iota(jnp.int32, (lines, half_width), 1)
        core, high, rest = line // (8 * ring), line // (4 * ring) % 2, line % (4 * ring)
        source = rest // 4 * (16 * rows_y) + core * (8 * rows_y) + to * 8 + high * 4 + rest % 4
        pick = jnp.where(column == source, 1.0, 0.0).astype(jnp.bfloat16)
        for lo in range(2):
            part = xin[:, lo * half_width : (lo + 1) * half_width]
            xt[t, lo] = lax.dot_general(
                pick, part, (((1,), (1,)), ((), ())), preferred_element_type=jnp.float32
            ).astype(jnp.bfloat16)

    loads = [
        pltpu.make_async_copy(src, dst, in_sem.at[i])
        for i, (src, dst) in enumerate(
            (
                (k_ref, near.at[0]), (v_ref, near.at[1]), (x_ref, xin), (q_ref, q), (g_ref, g),
            )
        )
    ]
    for load in loads:
        load.wait()
    for j in (1, 2, 3):
        want_copy(j).wait()
    table = pltpu.make_async_copy(wants, want_smem, smem_sem.at[0])
    table.start()
    table.wait()

    def slot_copy(part, j, r):
        owner = lax.rem(z + r, ring)
        return push(
            stage.at[part, r, j - 1], slots.at[part, pl.ds((cls * ring + owner) * CAP, CAP)],
            s_send.at[part, j - 1, r], s_recv.at[part, j - 1, r], member(ring, j)[0],
        )

    def extract(part, r, chunk):
        owner = lax.rem(z + r, ring)
        for b in range(2):
            for h in range(KV_HEADS):
                work[b * KV_HEADS + h] = chunk(b)[:, h * HEAD_WIDTH : (h + 1) * HEAD_WIDTH]
        for j in (2, 3, 1, 0):
            for rank in range(CAP):
                unit = jnp.maximum(want_smem[j, 0, owner * CAP + rank], 0)
                if j:
                    stage[part, r, j - 1, rank] = work[unit]
                else:
                    slots[part, (cls * ring + owner) * CAP + rank] = work[unit]
            if j == 1:
                slot_copy(part, j, r).start()
            elif j:
                pl.when(x == 0)(lambda: slot_copy(part, j, r).start())

    for part in range(2):
        extract(part, 0, lambda b: near[part, b * BLOCK_LENGTH : (b + 1) * BLOCK_LENGTH])
    for t in range(rows_y):
        deal(t)
        if t == 0:
            keep_copy().start()
        else:
            x_copy(t).start()

    def from_below(s, part):
        extract(part, ring - 1 - s, lambda b: up[s, part, b])

    def from_above(s, part):
        extract(part, 1 + s, lambda b: down[s, part, b])

    def relay(s, part, b, parts_up, parts_down):
        up_copy(s, part, b, some).wait_recv()
        if part in parts_up:
            up_copy(s + 1, part, b).start()
        down_copy(s, part, b, some).wait_recv()
        if part in parts_down:
            down_copy(s + 1, part, b).start()

    def step(s, _):
        relay(s, 0, 0, (0, 1), (0, 1))
        pl.when(s > 0)(lambda: from_above(s - 1, 1))
        pl.when(s < KV_HEADS)(lambda: local_part(s, 0))
        relay(s, 0, 1, (0, 1), (0, 1))
        from_below(s, 0)
        relay(s, 1, 0, (0, 1), (0, 1))
        from_above(s, 0)
        pl.when(s < KV_HEADS)(lambda: local_part(s, 1))
        relay(s, 1, 1, (0, 1), (0, 1))
        from_below(s, 1)
        return 0

    lax.fori_loop(0, half - 2, step, 0)
    s = half - 2
    relay(s, 0, 0, (0,), (1,))
    from_above(s - 1, 1)
    relay(s, 0, 1, (0,), (1,))
    from_below(s, 0)
    relay(s, 1, 0, (0,), (1,))
    from_above(s, 0)
    relay(s, 1, 1, (0,), (1,))
    from_below(s, 1)
    from_above(s, 1)
    for b in range(2):
        up_copy(half - 1, 0, b, some).wait_recv()
    extract(0, half, lambda b: up[half - 1, 0, b])
    for b in range(2):
        down_copy(half - 1, 1, b, some).wait_recv()
    extract(1, half, lambda b: down[half - 1, 1, b])

    def drain(s, _):
        for part in range(2):
            for b in range(2):
                up_copy(s, part, b, some).wait_send()
                down_copy(s, part, b, some).wait_send()
        return 0

    lax.fori_loop(0, half - 1, drain, 0)
    for b in range(2):
        up_copy(half - 1, 0, b, some).wait_send()
        down_copy(half - 1, 1, b, some).wait_send()

    def drain_slots(r, _):
        for part in range(2):
            slot_copy(part, 1, r).wait()
            for j in (2, 3):
                pl.when(x == 0)(lambda: slot_copy(part, j, r).wait_send())
                pl.when(x == 1)(lambda: slot_copy(part, j, r).wait_recv())
        return 0

    lax.fori_loop(0, ring, drain_slots, 0)
    keep_copy().wait()
    for t in range(1, rows_y):
        x_copy(t).wait()


NT = (((1,), (1,)), ((), ()))
TN = (((0,), (0,)), ((), ()))
SCALE = HEAD_WIDTH ** (-0.5)


def stat_lines(lse_ref, delta_ref, lines):
    for which, ref in enumerate((lse_ref, delta_ref)):
        stat = ref[...].astype(jnp.float32)
        for b in range(2):
            for h in range(KV_HEADS):
                at = slice(b * BLOCK_LENGTH, (b + 1) * BLOCK_LENGTH)
                pieces = [stat[h * GROUP + i : h * GROUP + i + 1, at] for i in range(GROUP)]
                lines[which, b * KV_HEADS + h] = jnp.concatenate(pieces, axis=1)


def stacked_rows(ref, h, b):
    rows = slice(b * BLOCK_LENGTH, (b + 1) * BLOCK_LENGTH)
    return jnp.concatenate(
        [ref[rows, wide(h * GROUP + i)] for i in range(GROUP)], axis=0
    )


def wide(i):
    if isinstance(i, int):
        return slice(i * HEAD_WIDTH, (i + 1) * HEAD_WIDTH)
    return pl.ds(pl.multiple_of(i * HEAD_WIDTH, HEAD_WIDTH), HEAD_WIDTH)


def score_grads(keys, values, queries, grads, mask, lse, delta):
    scores = lax.dot_general(keys, queries, NT, preferred_element_type=jnp.float32) * SCALE
    prob = jnp.where(mask, jnp.exp(scores - lse), 0.0)
    dprob = lax.dot_general(values, grads, NT, preferred_element_type=jnp.float32)
    return prob.astype(jnp.bfloat16), (prob * (dprob - delta)).astype(jnp.bfloat16)


def attend_local(h, b, near, q, g, lines, dk, dv, dq_local):
    unit = b * KV_HEADS + h
    local = (b + 1) * BLOCK_LENGTH
    queries, grads = stacked_rows(q, h, b), stacked_rows(g, h, b)
    keys, values = near[0, :local, wide(h)], near[1, :local, wide(h)]
    shape = (local, GROUP * BLOCK_LENGTH)
    row = lax.broadcasted_iota(jnp.int32, shape, 1) % BLOCK_LENGTH + b * BLOCK_LENGTH
    mask = lax.broadcasted_iota(jnp.int32, shape, 0) <= row
    prob, dscore = score_grads(
        keys, values, queries, grads, mask, lines[0, unit], lines[1, unit]
    )
    dq_local[unit] = lax.dot_general(dscore, keys, TN, preferred_element_type=jnp.float32)
    key_part = jnp.dot(dscore, queries, preferred_element_type=jnp.float32) * SCALE
    value_part = jnp.dot(prob, grads, preferred_element_type=jnp.float32)
    for out, grad in ((dk, key_part), (dv, value_part)):
        if b == 0:
            out[:BLOCK_LENGTH, wide(h)] = grad
        else:
            out[:BLOCK_LENGTH, wide(h)] += grad[:BLOCK_LENGTH]
            out[BLOCK_LENGTH:, wide(h)] = grad[BLOCK_LENGTH:]


def chosen_rows(slots, meta, part, first):
    return jnp.concatenate(
        [slots[part, meta[first + i]] for i in range(CHOSEN_BLOCKS)], axis=0
    )


def attend_keys(meta, slots, q, g, lines, parts, probs, dscores):
    shape = (CHOSEN_BLOCKS * BLOCK_LENGTH, GROUP * BLOCK_LENGTH)
    key = lax.broadcasted_iota(jnp.int32, shape, 0)
    for b in range(2):
        for h in range(KV_HEADS):
            unit = b * KV_HEADS + h
            first = unit * CHOSEN_BLOCKS
            keys, values = (chosen_rows(slots, meta, part, first) for part in range(2))
            queries, grads = stacked_rows(q, h, b), stacked_rows(g, h, b)
            mask = None
            for i in range(CHOSEN_BLOCKS):
                begin = i * BLOCK_LENGTH
                limit = jnp.where(meta[64 + first + i] > 0, begin + BLOCK_LENGTH, begin)
                inside = (key >= begin) & (key < limit)
                mask = inside if mask is None else mask | inside
            prob, dscore = score_grads(
                keys, values, queries, grads, mask, lines[0, unit], lines[1, unit]
            )
            probs[unit] = prob
            dscores[unit] = dscore
            grad = (jnp.dot(dscore, queries, preferred_element_type=jnp.float32) * SCALE).astype(
                jnp.bfloat16
            )
            for i in range(CHOSEN_BLOCKS):
                parts[0, first + i] = grad[i * BLOCK_LENGTH : (i + 1) * BLOCK_LENGTH]


def attend_rest(meta, slots, g, parts, probs, dscores, dq_local, dq_ref):
    for b in range(2):
        for h in range(KV_HEADS):
            unit = b * KV_HEADS + h
            first = unit * CHOSEN_BLOCKS
            grad = jnp.dot(
                probs[unit], stacked_rows(g, h, b), preferred_element_type=jnp.float32
            ).astype(jnp.bfloat16)
            for i in range(CHOSEN_BLOCKS):
                parts[1, first + i] = grad[i * BLOCK_LENGTH : (i + 1) * BLOCK_LENGTH]
            keys = chosen_rows(slots, meta, 0, first)
            dq = dq_local[unit] + lax.dot_general(
                dscores[unit], keys, TN, preferred_element_type=jnp.float32
            )
            dq = (dq * SCALE).astype(jnp.bfloat16)
            for i in range(GROUP):
                dq_ref[b * BLOCK_LENGTH : (b + 1) * BLOCK_LENGTH, wide(h * GROUP + i)] = dq[
                    i * BLOCK_LENGTH : (i + 1) * BLOCK_LENGTH
                ]


def reduce_stage(
    ring, rows_y, weight_scale, part_ref, want_smem, index_smem, dk_ref, dv_ref, xg_ref,
    kg_ref, vg_ref, wg_ref,
    up, down, ups, downs, arrived, stage, mine,
    all_k, own, across, shared, to_x, from_x, pieces, to_z, from_z,
    up_send, up_recv, down_send, down_recv, s_send, s_recv,
    y_send, y_recv, c_send, c_recv, x_send, x_recv, z_send, z_recv, rest,
):
    half = ring // 2
    x, z, c = place(ring)
    high = lax.rem(lax.axis_index("dp"), 2)
    cls = x * 2 + c
    above, below = along(ring, 1), along(ring, -1)

    def slot_copy(part, j, r):
        return push(
            stage.at[part, j - 1, r], arrived.at[part, j - 1, r],
            s_send.at[part, j - 1, r], s_recv.at[part, j - 1, r], member(ring, j)[0],
        )

    def term_of(part, line, owner, rank):
        return part_ref[part, index_smem[line, 0, owner * CAP + rank]]

    def send_slots(part, r):
        owner = lax.rem(z + r, ring)

        def send(j):
            line = member(ring, j)[1]
            for rank in range(CAP):
                stage[part, j - 1, r, rank] = term_of(part, line, owner, rank)
            slot_copy(part, j, r).start()

        for j in (2, 3):
            pl.when(x == 1)(lambda: send(j))
        send(1)

    def below_of(act, part, s):
        pl.when((s >= 0) & (s <= half))(lambda: act(part, half - s))

    def above_of(act, part, s):
        pl.when((s > 0) & (s < half))(lambda: act(part, half + s))

    def up_copy(part, s, b):
        return push(
            ups.at[part, s, b], up.at[part, s, b], up_send.at[part, s, b], up_recv.at[part, s, b], above
        )

    def down_copy(part, s, b):
        return push(
            downs.at[part, s, b], down.at[part, s, b],
            down_send.at[part, s, b], down_recv.at[part, s, b], below,
        )

    def gather_terms(part, r):
        owner = lax.rem(z + r, ring)

        def add(mates, before):
            units = [[want_smem[j, 0, owner * CAP + rank] for rank in range(CAP)] for j in mates]
            for b in range(2):
                for h in range(KV_HEADS):
                    at = (part, r, b, slice(None), slice(h * HEAD_WIDTH, (h + 1) * HEAD_WIDTH))
                    acc = mine[at] if before else jnp.zeros((BLOCK_LENGTH, HEAD_WIDTH), jnp.float32)
                    for j, asked in zip(mates, units, strict=True):
                        for rank in range(CAP):
                            if j == 0:
                                term = term_of(part, cls, owner, rank)
                            else:
                                term = arrived[part, j - 1, r, rank]
                            hit = asked[rank] == b * KV_HEADS + h
                            acc = acc + jnp.where(hit, term.astype(jnp.float32), 0.0)
                    mine[at] = acc

        slot_copy(part, 1, r).wait_recv()
        add((0, 1), False)

        @pl.when(x == 0)
        def _():
            for j in (2, 3):
                slot_copy(part, j, r).wait_recv()
            add((2, 3), True)

    def first(part, d):
        copy, outgoing = ((up_copy, ups), (down_copy, downs))[d]
        outgoing[part, 0, d] = mine[part, half, d].astype(jnp.bfloat16)
        copy(part, 0, d).start()

    def hop(part, s, d, b):
        copy, arrival, outgoing = ((up_copy, up, ups), (down_copy, down, downs))[d]
        r = half + s if d else half - s
        if d == b:
            copy(part, s - 1, b).wait_recv()
        else:
            pl.when(s > 1)(lambda: copy(part, s - 1, b).wait_recv())
        value = arrival[part, s - 1, b].astype(jnp.float32) + mine[part, r, b]
        outgoing[part, s, b] = value.astype(jnp.bfloat16)
        copy(part, s, b).start()

    def last(part):
        near, outs = ((dk_ref, (kg_ref, own)), (dv_ref, (vg_ref,)))[part]
        for b in range(2):
            up_copy(part, half - 1, b).wait_recv()
            down_copy(part, half - 1, b).wait_recv()
            rows = slice(b * BLOCK_LENGTH, (b + 1) * BLOCK_LENGTH)
            value = near[rows] + mine[part, 0, b]
            value = value + up[part, half - 1, b].astype(jnp.float32)
            value = value + down[part, half - 1, b].astype(jnp.float32)
            for out in outs:
                out[rows] = value.astype(jnp.bfloat16)

    send_slots(0, half)
    for s in range(1, AHEAD + 1):
        send_slots(0, half - s)
        send_slots(0, half + s)
    blank = jnp.zeros((BLOCK_LENGTH, KV_HEADS * HEAD_WIDTH), jnp.bfloat16)
    for part in range(2):
        up[part, 0, 1] = blank
        down[part, 0, 0] = blank

    y = lax.axis_index("dp") // 2

    def y_copy(t):
        return push(own, all_k.at[y], y_send.at[t - 1], y_recv.at[t - 1], column_mate(t))

    def c_copy():
        return push(across.at[:, 1 - c], shared, c_send, c_recv, member(ring, 1)[0])

    def x_copy(j):
        mate, lo, hi = row_mate(ring, j)
        return push(
            to_x.at[lo, hi], from_x.at[j - 1], x_send.at[j - 1], x_recv.at[j - 1], mate
        )

    def z_copy(d):
        return push(
            to_z.at[lax.rem(z + d, ring)], from_z.at[d - 1],
            z_send.at[d - 1], z_recv.at[d - 1], along(ring, d),
        )

    def start_weights():
        for t in range(1, rows_y):
            y_copy(t).start()
        all_k[y] = own[...]

    def multiply():
        for t in range(1, rows_y):
            y_copy(t).wait_recv()
        gathered = all_k[...].reshape(rows_y * TOKENS, KV_HEADS * HEAD_WIDTH)
        for lo in range(2):
            product = jnp.dot(xg_ref[lo], gathered, preferred_element_type=jnp.float32)
            for core in range(2):
                for hi in range(2):
                    begin = (core * 2 + hi) * 4 * ring
                    across[lo, core, hi] = product[begin : begin + 4 * ring]
        c_copy().start()

    def add_core():
        c_copy().wait()
        for lo in range(2):
            for hi in range(2):
                value = across[lo, c, hi] + shared[lo, hi]
                across[lo, c, hi] = value
                to_x[lo, hi] = value.astype(jnp.bfloat16)
        for j in (1, 2, 3):
            x_copy(j).start()

    def add_row():
        for j in (1, 2, 3):
            x_copy(j).wait()
        value = across[x, c, high]
        for j in range(3):
            value = value + from_x[j].astype(jnp.float32)
        for i in range(ring):
            piece = value[4 * i : 4 * i + 4]
            pieces[i] = piece
            to_z[i] = jnp.concatenate([piece[:, wide(n)] for n in range(KV_HEADS)], axis=0).astype(
                jnp.bfloat16
            )
        for d in range(1, ring):
            z_copy(d).start()

    rest()
    gather_terms(0, half)
    first(0, 0)
    first(0, 1)
    gather_terms(0, half - 1)
    gather_terms(0, half + 1)
    jobs = (
        (half, start_weights), (half + MULTIPLY, multiply), (half + ADD_CORE, add_core),
        (half + ADD_ROW, add_row),
    )
    end = half + LAG

    def step(t, _):
        behind = t - LAG
        fillers = (
            (below_of, send_slots, AHEAD, AHEAD_V), (above_of, send_slots, AHEAD, AHEAD_V),
            (below_of, gather_terms, 1, 1), (above_of, gather_terms, 1, 1),
        )
        for (d, b), (of, act, lead, lead_v) in zip(((0, 0), (1, 1), (0, 1), (1, 0)), fillers, strict=True):
            pl.when(t < half)(lambda: hop(0, t, d, b))
            of(act, 0, t + lead)
            if d == b:
                pl.when(behind == 0)(lambda: first(1, d))
            pl.when(behind > 0)(lambda: hop(1, behind, d, b))
            of(act, 1, behind + lead_v)
        pl.when(t == half)(lambda: last(0))
        for at, act in jobs:
            pl.when(t == at)(act)
        return 0

    lax.fori_loop(1, end, step, 0)
    last(1)
    for at, act in jobs:
        if at >= end:
            act()
    value = jnp.zeros(from_z.shape[1:], jnp.float32)
    for d in range(1, ring):
        z_copy(d).wait_recv()
        value = value + from_z[d - 1].astype(jnp.float32)
    value = jnp.concatenate([value[4 * n : 4 * n + 4] for n in range(KV_HEADS)], axis=1)
    wg_ref[...] = (pieces[z] + value) * weight_scale

    for t in range(1, rows_y):
        y_copy(t).wait_send()
    for d in range(1, ring):
        z_copy(d).wait_send()
    for part in range(2):
        up_copy(part, 0, 0).wait_send()
        down_copy(part, 0, 1).wait_send()

        def drain(s, _):
            for b in range(2):
                up_copy(part, s, b).wait_send()
                down_copy(part, s, b).wait_send()
            return 0

        lax.fori_loop(1, half, drain, 0)

        def drain_slots(r, _):
            slot_copy(part, 1, r).wait_send()
            for j in (2, 3):
                pl.when(x == 1)(lambda: slot_copy(part, j, r).wait_send())
            return 0

        lax.fori_loop(0, ring, drain_slots, 0)


def fused_kernel(
    ring, rows_y, weight_scale, chosen_ref, k_ref, v_ref, x_ref, q_ref, g_ref, lse_ref, delta_ref,
    dq_ref, kg_ref, vg_ref, wg_ref,
    slots, wants, index, meta, want_smem, index_smem, xg, near, q, g, dk, dv, parts,
    lines, dq_local, probs, dscores,
    in_sem, smem_sem, *scratch,
):
    loads = [
        pltpu.make_async_copy(src, dst, in_sem.at[i])
        for i, (src, dst) in enumerate(
            (
                (k_ref, near.at[0]), (v_ref, near.at[1]), (x_ref, scratch[GATHER_INPUT]),
                (q_ref, q), (g_ref, g),
            )
        )
    ]
    for load in loads:
        load.start()
    far_x = [row_mate(ring, j)[0] for j in (1, 3)]
    far_z = [{"ctx": along(ring, d)} for d in range(2, ring - 1)]
    stat_lines(lse_ref, delta_ref, lines)
    greet(neighbours(ring) + [column_mate(t) for t in range(1, rows_y)] + far_x + far_z)
    gather_stage(
        ring, rows_y, chosen_ref, k_ref, v_ref, x_ref, q_ref, g_ref, q, g, slots, wants, index, meta, want_smem, xg, near,
        *scratch[:GATHER_SCRATCH], smem_sem, in_sem,
        lambda h, b: attend_local(h, b, near, q, g, lines, dk, dv, dq_local),
    )
    table = pltpu.make_async_copy(index, index_smem, smem_sem.at[1])
    table.start()
    attend_keys(meta, slots, q, g, lines, parts, probs, dscores)
    table.wait()
    reduce_stage(
        ring, rows_y, weight_scale, parts, want_smem, index_smem, dk, dv, xg,
        kg_ref, vg_ref, wg_ref, *scratch[GATHER_SCRATCH:],
        lambda: attend_rest(meta, slots, g, parts, probs, dscores, dq_local, dq_ref),
    )


def fused_call(ring, rows_y, weight_scale, chosen, keys, values, inputs, queries, grads, lse, delta):
    half = ring // 2
    lines = 16 * ring
    width = KV_HEADS * HEAD_WIDTH
    number = 2 * KV_HEADS * CHOSEN_BLOCKS
    hbm, vmem = pl.BlockSpec(memory_space=pl.ANY), pl.BlockSpec(memory_space=pltpu.VMEM)
    smem = pl.BlockSpec(memory_space=pltpu.SMEM)
    dma = pltpu.SemaphoreType.DMA
    low, full = jnp.bfloat16, jnp.float32
    table = (4, 8, 128)
    shared = [
        pltpu.VMEM((2, 4 * ring * CAP, BLOCK_LENGTH, HEAD_WIDTH), low),
        pltpu.VMEM(table, jnp.int32),
        pltpu.VMEM(table, jnp.int32),
        pltpu.SMEM((128,), jnp.int32),
        pltpu.SMEM(table, jnp.int32),
        pltpu.SMEM(table, jnp.int32),
        pltpu.VMEM((2, lines, rows_y * TOKENS), low),
        pltpu.VMEM((2,) + keys.shape, low),
        pltpu.VMEM(queries.shape, low),
        pltpu.VMEM(queries.shape, low),
        pltpu.VMEM(keys.shape, full),
        pltpu.VMEM(keys.shape, full),
        pltpu.VMEM((2, number, BLOCK_LENGTH, HEAD_WIDTH), low),
        pltpu.VMEM((2, UNITS, 1, GROUP * BLOCK_LENGTH), full),
        pltpu.VMEM((UNITS, GROUP * BLOCK_LENGTH, HEAD_WIDTH), full),
        pltpu.VMEM((UNITS, CHOSEN_BLOCKS * BLOCK_LENGTH, GROUP * BLOCK_LENGTH), low),
        pltpu.VMEM((UNITS, CHOSEN_BLOCKS * BLOCK_LENGTH, GROUP * BLOCK_LENGTH), low),
        dma((5,)), dma((2,)),
    ]
    gather_ring = pltpu.VMEM((half, 2, 2, BLOCK_LENGTH, width), low)
    gather_sem = dma((half, 2, 2))
    gather = [
        gather_ring, gather_ring,
        pltpu.VMEM((2, ring, 3, CAP, BLOCK_LENGTH, HEAD_WIDTH), low),
        pltpu.VMEM((UNITS, BLOCK_LENGTH, HEAD_WIDTH), low),
        pltpu.VMEM(table, jnp.int32),
        pltpu.VMEM((rows_y, 2, lines, TOKENS), low),
        pltpu.VMEM(inputs.shape, low),
        gather_sem, gather_sem, gather_sem, gather_sem,
        dma((3,)), dma((3,)), dma((2, 3, ring)), dma((2, 3, ring)), dma((rows_y,)), dma((rows_y,)),
    ]
    reduce_ring, reduce_sem = pltpu.VMEM((2, half, 2, BLOCK_LENGTH, width), low), dma((2, half, 2))
    reduce = [
        reduce_ring, reduce_ring, reduce_ring, reduce_ring,
        pltpu.VMEM((2, 3, ring, CAP, BLOCK_LENGTH, HEAD_WIDTH), low),
        pltpu.VMEM((2, 3, ring, CAP, BLOCK_LENGTH, HEAD_WIDTH), low),
        pltpu.VMEM((2, ring, 2, BLOCK_LENGTH, width), full),
        pltpu.VMEM((rows_y, TOKENS, width), low),
        pltpu.VMEM((TOKENS, width), low),
        pltpu.VMEM((2, 2, 2, 4 * ring, width), full),
        pltpu.VMEM((2, 2, 4 * ring, width), full),
        pltpu.VMEM((2, 2, 4 * ring, width), low),
        pltpu.VMEM((3, 4 * ring, width), low),
        pltpu.VMEM((ring, 4, width), full),
        pltpu.VMEM((ring, 4 * KV_HEADS, HEAD_WIDTH), low),
        pltpu.VMEM((ring - 1, 4 * KV_HEADS, HEAD_WIDTH), low),
        reduce_sem, reduce_sem, reduce_sem, reduce_sem,
        dma((2, 3, ring)), dma((2, 3, ring)),
        dma((rows_y - 1,)), dma((rows_y - 1,)), dma, dma,
        dma((3,)), dma((3,)), dma((ring - 1,)), dma((ring - 1,)),
    ]
    assert len(gather) == GATHER_SCRATCH
    return pl.pallas_call(
        functools.partial(fused_kernel, ring, rows_y, weight_scale),
        out_shape=(
            jax.ShapeDtypeStruct(queries.shape, low),
            jax.ShapeDtypeStruct((TOKENS, width), low),
            jax.ShapeDtypeStruct((TOKENS, width), low),
            jax.ShapeDtypeStruct((4, width), full),
        ),
        in_specs=[smem, hbm, hbm, hbm, hbm, hbm, vmem, vmem],
        out_specs=(vmem,) * 4,
        scratch_shapes=shared + gather + reduce,
        compiler_params=pltpu.CompilerParams(
            collective_id=0, has_side_effects=True, vmem_limit_bytes=VMEM_BYTES
        ),
        name="fused_blocks",
    )(chosen, keys, values, inputs, queries, grads, lse, delta)


def hand_over_kernel(*refs):
    n = len(refs) // 2
    for i in range(n):
        refs[n + i][...] = refs[i][...]


def hand_over(*arrays):
    vmem = pl.BlockSpec(memory_space=pltpu.VMEM)
    return pl.pallas_call(
        hand_over_kernel,
        in_specs=[vmem] * len(arrays),
        out_specs=(vmem,) * len(arrays),
        out_shape=tuple(jax.ShapeDtypeStruct(a.shape, a.dtype) for a in arrays),
        name="hand_over",
    )(*arrays)


def body(
    query_states,
    key_activations,
    value_activations,
    out_grad,
    logsumexp,
    row_delta,
    layer_input,
    chosen,
):
    shards = lax.axis_size("ctx")
    replicas = lax.axis_size("dp")
    ring = shards // 4
    rows_y = replicas // 2
    keys, values = key_activations[0], value_activations[0]
    weight_scale = 1.0 / math.sqrt(TOKENS * shards * replicas)
    outputs = fused_call(
        ring, rows_y, weight_scale, chosen[0], keys, values, layer_input[0],
        query_states[0], out_grad[0], logsumexp[0], row_delta[0],
    )
    query_grad, key_gradient, value_gradient, key_weight_grad = hand_over(*outputs)
    return (query_grad[None], key_gradient[None], value_gradient[None], key_weight_grad)


def solution(mesh):
    seq = P("dp", "ctx", None)
    stat = P("dp", None, "ctx")
    return jax.shard_map(
        body,
        mesh=mesh,
        in_specs=(seq, seq, seq, seq, stat, stat, seq, P("dp", "ctx", None, None)),
        out_specs=(seq, seq, seq, P(("ctx", "dp"), None)),
        check_vma=False,
    )
```

time: 150 us -> 145 us (0.967)
  Pallas kernels: 148 us -> 143 us
    pallas_call x1, Pallas kernels: 146 us -> 141 us  [fused_call(): pl.pallas_call(functools.partial(fused_kernel, ring, rows_y, weight_scale...]
where the time goes in v5:
time: 145 us
  Pallas kernels  143 us (99%)
    pallas_call x1, Pallas kernels, fused_call(): pl.pallas_call(functools.partial(fused_kernel, ring, rows_y, weight_scale...  141 us

profile of v5, /device:TPU:24, one launch (start us, length us, event | category | flops | bytes accessed | tf_op | source)
XLA Modules:
  0.0 144.9 jit_solution(13423810628745730980)
XLA Ops:
  0.6 0.0 copy-start
  0.6 0.7 copy-done
  1.3 0.7 copy.12.chosen_ref
  2.0 140.9 %fused_blocks.1 = (bf16[128,2048]{1,0:T(8,128)(2,1)}, bf16[128,512]{1,0:T(8,128)(2,1)}, bf16[128,512]{1,0:T(8,128)(2,1)}, f32[4,512]{1,0:T(4,128)}) custom-call(s32[2,4,3]{2,1,0:T(4,128)} %copy.12.chosen_ref, bf16[128,512]{1,0:T(8,128)(2,1)} %bitcast.14, bf16[128,512]{1,0:T(8,128)(2,1)} %bitcast.15, bf16[128,2048]{1,0:T(8,128)(2,1)} %bitcast.11, ...), custom_call_target="tpu_custom_call" | custom-call | tf_op jit(solution)/shard_map/fused_blocks/pallas_call | solution.py:746
  142.9 2.0 %hand_over.1 = (bf16[128,2048]{1,0:T(8,128)(2,1)}, bf16[128,512]{1,0:T(8,128)(2,1)}, bf16[128,512]{1,0:T(8,128)(2,1)}, f32[4,512]{1,0:T(4,128)}) custom-call(bf16[128,2048]{1,0:T(8,128)(2,1)} %get-tuple-element.12.refs_0_, bf16[128,512]{1,0:T(8,128)(2,1)} %get-tuple-element.13.refs_1_, bf16[128,512]{1,0:T(8,128)(2,1)} %get-tuple-element.14.refs_2_, ...), custom_call_target="tpu_custom_call" | custom-call | tf_op jit(solution)/shard_map/hand_over/pallas_call | solution.py:772
Async XLA Ops:
  0.6 0.7 copy-start

commit v6 on v5

--- a/solution.py
+++ b/solution.py
@@ -55,10 +55,11 @@
     return {"ctx": lo * (2 * ring) + z * 2 + c, "dp": d // 2 * 2 + hi}, lo, hi
 
 
-def greet(others):
+def greet(others, meanwhile):
     barrier = pltpu.get_barrier_semaphore()
     for other in others:
         pl.semaphore_signal(barrier, inc=1, device_id=other, device_id_type=MESH)
+    meanwhile()
     pl.semaphore_wait(barrier, len(others))
 
 
@@ -109,7 +110,8 @@
     spots = jnp.zeros(shape, jnp.int32)
     owners = []
     for i in range(2 * KV_HEADS * CHOSEN_BLOCKS):
-        choice = chosen_ref[i // (KV_HEADS * CHOSEN_BLOCKS), i // CHOSEN_BLOCKS % KV_HEADS, i % CHOSEN_BLOCKS]
+        b, h = i // (KV_HEADS * CHOSEN_BLOCKS), i // CHOSEN_BLOCKS % KV_HEADS
+        choice = chosen_ref[0, i % CHOSEN_BLOCKS, b, h]
         active = choice >= 0
         block = jnp.maximum(choice, 0)
         owner = block // 2
@@ -646,7 +648,7 @@
     ring, rows_y, weight_scale, chosen_ref, k_ref, v_ref, x_ref, q_ref, g_ref, lse_ref, delta_ref,
     dq_ref, kg_ref, vg_ref, wg_ref,
     slots, wants, index, meta, want_smem, index_smem, xg, near, q, g, dk, dv, parts,
-    lines, dq_local, probs, dscores,
+    lines, dq_local, probs, dscores, chosen_smem,
     in_sem, smem_sem, *scratch,
 ):
     loads = [
@@ -660,12 +662,17 @@
     ]
     for load in loads:
         load.start()
+    choices = pltpu.make_async_copy(chosen_ref, chosen_smem, in_sem.at[5])
+    choices.start()
     far_x = [row_mate(ring, j)[0] for j in (1, 3)]
     far_z = [{"ctx": along(ring, d)} for d in range(2, ring - 1)]
-    stat_lines(lse_ref, delta_ref, lines)
-    greet(neighbours(ring) + [column_mate(t) for t in range(1, rows_y)] + far_x + far_z)
+    greet(
+        neighbours(ring) + [column_mate(t) for t in range(1, rows_y)] + far_x + far_z,
+        lambda: stat_lines(lse_ref, delta_ref, lines),
+    )
+    choices.wait()
     gather_stage(
-        ring, rows_y, chosen_ref, k_ref, v_ref, x_ref, q_ref, g_ref, q, g, slots, wants, index, meta, want_smem, xg, near,
+        ring, rows_y, chosen_smem, k_ref, v_ref, x_ref, q_ref, g_ref, q, g, slots, wants, index, meta, want_smem, xg, near,
         *scratch[:GATHER_SCRATCH], smem_sem, in_sem,
         lambda h, b: attend_local(h, b, near, q, g, lines, dk, dv, dq_local),
     )
@@ -686,7 +693,6 @@
     width = KV_HEADS * HEAD_WIDTH
     number = 2 * KV_HEADS * CHOSEN_BLOCKS
     hbm, vmem = pl.BlockSpec(memory_space=pl.ANY), pl.BlockSpec(memory_space=pltpu.VMEM)
-    smem = pl.BlockSpec(memory_space=pltpu.SMEM)
     dma = pltpu.SemaphoreType.DMA
     low, full = jnp.bfloat16, jnp.float32
     table = (4, 8, 128)
@@ -708,7 +714,8 @@
         pltpu.VMEM((UNITS, GROUP * BLOCK_LENGTH, HEAD_WIDTH), full),
         pltpu.VMEM((UNITS, CHOSEN_BLOCKS * BLOCK_LENGTH, GROUP * BLOCK_LENGTH), low),
         pltpu.VMEM((UNITS, CHOSEN_BLOCKS * BLOCK_LENGTH, GROUP * BLOCK_LENGTH), low),
-        dma((5,)), dma((2,)),
+        pltpu.SMEM(chosen.shape, jnp.int32),
+        dma((6,)), dma((2,)),
     ]
     gather_ring = pltpu.VMEM((half, 2, 2, BLOCK_LENGTH, width), low)
     gather_sem = dma((half, 2, 2))
@@ -751,7 +758,7 @@
             jax.ShapeDtypeStruct((TOKENS, width), low),
             jax.ShapeDtypeStruct((4, width), full),
         ),
-        in_specs=[smem, hbm, hbm, hbm, hbm, hbm, vmem, vmem],
+        in_specs=[hbm, hbm, hbm, hbm, hbm, hbm, vmem, vmem],
         out_specs=(vmem,) * 4,
         scratch_shapes=shared + gather + reduce,
         compiler_params=pltpu.CompilerParams(
@@ -795,7 +802,7 @@
     keys, values = key_activations[0], value_activations[0]
     weight_scale = 1.0 / math.sqrt(TOKENS * shards * replicas)
     outputs = fused_call(
-        ring, rows_y, weight_scale, chosen[0], keys, values, layer_input[0],
+        ring, rows_y, weight_scale, chosen.transpose(0, 3, 1, 2), keys, values, layer_input[0],
         query_states[0], out_grad[0], logsumexp[0], row_delta[0],
     )
     query_grad, key_gradient, value_gradient, key_weight_grad = hand_over(*outputs)

time: 145 us -> 144 us (level)
  no operation moved by 1% of the time
where the time goes in v6:
time: 144 us
  Pallas kernels  143 us (99%)
    pallas_call x1, Pallas kernels, fused_call(): pl.pallas_call(functools.partial(fused_kernel, ring, rows_y, weight_scale...  141 us

profile of v6, /device:TPU:24, one launch (start us, length us, event | category | flops | bytes accessed | tf_op | source)
XLA Modules:
  0.0 143.5 jit_solution(12891798128092814631)
XLA Ops:
  0.6 140.9 %fused_blocks.1 = (bf16[128,2048]{1,0:T(8,128)(2,1)}, bf16[128,512]{1,0:T(8,128)(2,1)}, bf16[128,512]{1,0:T(8,128)(2,1)}, f32[4,512]{1,0:T(4,128)}) custom-call(s32[1,3,2,4]{3,2,1,0:T(2,128)} %bitcast.18, bf16[128,512]{1,0:T(8,128)(2,1)} %bitcast.14, bf16[128,512]{1,0:T(8,128)(2,1)} %bitcast.15, bf16[128,2048]{1,0:T(8,128)(2,1)} %bitcast.11, ...), custom_call_target="tpu_custom_call" | custom-call | tf_op jit(solution)/shard_map/fused_blocks/pallas_call | solution.py:753
  141.5 2.0 %hand_over.1 = (bf16[128,2048]{1,0:T(8,128)(2,1)}, bf16[128,512]{1,0:T(8,128)(2,1)}, bf16[128,512]{1,0:T(8,128)(2,1)}, f32[4,512]{1,0:T(4,128)}) custom-call(bf16[128,2048]{1,0:T(8,128)(2,1)} %get-tuple-element.12.refs_0_, bf16[128,512]{1,0:T(8,128)(2,1)} %get-tuple-element.13.refs_1_, bf16[128,512]{1,0:T(8,128)(2,1)} %get-tuple-element.14.refs_2_, ...), custom_call_target="tpu_custom_call" | custom-call | tf_op jit(solution)/shard_map/hand_over/pallas_call | solution.py:779

commit v7 on v6

--- a/solution.py
+++ b/solution.py
@@ -16,7 +16,7 @@
 GROUP = 4
 TOKENS = 128
 UNITS = TOKENS // BLOCK_LENGTH * KV_HEADS
-LAG = 5
+LAG = 6
 AHEAD = 4
 AHEAD_V = 4
 MULTIPLY, ADD_CORE, ADD_ROW = 2, 3, 4

time: 144 us -> 143 us (level)
  no operation moved by 1% of the time
where the time goes in v7:
time: 143 us
  Pallas kernels  142 us (99%)
    pallas_call x1, Pallas kernels, fused_call(): pl.pallas_call(functools.partial(fused_kernel, ring, rows_y, weight_scale...  140 us

profile of v7, /device:TPU:24, one launch (start us, length us, event | category | flops | bytes accessed | tf_op | source)
XLA Modules:
  0.0 142.7 jit_solution(7616548307328879703)
XLA Ops:
  0.6 140.0 %fused_blocks.1 = (bf16[128,2048]{1,0:T(8,128)(2,1)}, bf16[128,512]{1,0:T(8,128)(2,1)}, bf16[128,512]{1,0:T(8,128)(2,1)}, f32[4,512]{1,0:T(4,128)}) custom-call(s32[1,3,2,4]{3,2,1,0:T(2,128)} %bitcast.18, bf16[128,512]{1,0:T(8,128)(2,1)} %bitcast.14, bf16[128,512]{1,0:T(8,128)(2,1)} %bitcast.15, bf16[128,2048]{1,0:T(8,128)(2,1)} %bitcast.11, ...), custom_call_target="tpu_custom_call" | custom-call | tf_op jit(solution)/shard_map/fused_blocks/pallas_call | solution.py:753
  140.7 2.0 %hand_over.1 = (bf16[128,2048]{1,0:T(8,128)(2,1)}, bf16[128,512]{1,0:T(8,128)(2,1)}, bf16[128,512]{1,0:T(8,128)(2,1)}, f32[4,512]{1,0:T(4,128)}) custom-call(bf16[128,2048]{1,0:T(8,128)(2,1)} %get-tuple-element.12.refs_0_, bf16[128,512]{1,0:T(8,128)(2,1)} %get-tuple-element.13.refs_1_, bf16[128,512]{1,0:T(8,128)(2,1)} %get-tuple-element.14.refs_2_, ...), custom_call_target="tpu_custom_call" | custom-call | tf_op jit(solution)/shard_map/hand_over/pallas_call | solution.py:779
